TPU v7x, 32 devices: a whole 2x2x4 slice. The times are simulated.
32 devices in a mesh: rep: 8 (over z, y), blk: 4 (over x, core).
Axes of the slice: x: 2, y: 2, z: 4, core: 2. Of those that a mesh axis runs over, the one named last changes fastest.
Arguments:
- encoded: bfloat16 [128, 512, 512], P(('rep', 'blk')), may hold values from -6 to 6
- queries: bfloat16 [1024, 512], P('blk'), may hold values from -0.25 to 0.25
- classifiers: bfloat16 [1024, 512], P('blk'), may hold values from -1 to 1
- lengths: int32 [128], P(('rep', 'blk')), may hold values from 1 to 512, 49152 in all
- beam: int32 [128, 1024], P(('rep', 'blk')), may hold values 0 or 1
- logit_grad: float32 [128, 1024], P(('rep', 'blk')), may hold values from -6 to 6
Outputs:
- logits: float32 [128, 1024], P(('rep', 'blk'))
- encoded_grad: bfloat16 [128, 512, 512], P(('rep', 'blk'))
- label_grad: float32 [1024, 1024], P('blk')
Inputs may be any that keep to these rules, and one draw needn't show every extreme that they name: `lengths`: every document has at least one real token, and some document has exactly 512.
All inputs are finite; a program needn't handle non-finite values. No bound on the sum of `lengths` or of `beam` on one device may be relied on, other than what follows from the above.
Results may differ from a plain program's by a relative error of at most 0.0058.
Values may be sent and summed in bfloat16 or wider, within the bound.
No kernel may reach another device: no remote copies, remote signals or barrier semaphores. Data moves between devices by JAX's collectives and lax.ppermute only.
A program may use at most 64 MiB of HBM per device.

v0:
```python
import functools

import jax
import jax.numpy as jnp
from jax import lax
from jax.experimental import pallas as pl
from jax.experimental.pallas import tpu as pltpu
from jax.sharding import PartitionSpec as P

F32 = jnp.float32
BF16 = jnp.bfloat16
VMEM = pl.BlockSpec(memory_space=pltpu.VMEM)
SMEM = pl.BlockSpec(memory_space=pltpu.SMEM)
HBM = pl.BlockSpec(memory_space=pltpu.HBM)
PARAMS = pltpu.CompilerParams(vmem_limit_bytes=20 * 1024 * 1024)
GROUP = 4
LANES = 128
EXTRA = 16


LONG = pl.CostEstimate(flops=10**11, transcendentals=0, bytes_accessed=0)


def shape(dims, dtype):
    return jax.ShapeDtypeStruct(dims, dtype)


def mm(a, b):
    return jnp.dot(a, b, preferred_element_type=F32)


def cost(products, docs, tokens, width, labels):
    return pl.CostEstimate(
        flops=2 * products * docs * tokens * width * labels,
        transcendentals=docs * tokens * labels,
        bytes_accessed=4 * docs * tokens * width,
    )


def call(kernel, out_shape, ins, name, scratch=(), estimate=None, hbm=0):
    single = not isinstance(out_shape, (list, tuple))
    ins = [pltpu.with_memory_space_constraint(x, pltpu.HBM) for x in ins[:hbm]] + list(ins[hbm:])
    return pl.pallas_call(
        kernel,
        out_shape=out_shape,
        in_specs=[
            HBM if i < hbm else SMEM if x.ndim == 1 else VMEM for i, x in enumerate(ins)
        ],
        out_specs=VMEM if single else [VMEM] * len(out_shape),
        scratch_shapes=scratch,
        compiler_params=PARAMS,
        cost_estimate=estimate,
        name=name,
    )(*ins)


def lanes_of(k, labels):
    return pl.ds(pl.multiple_of((lax.axis_index("blk") ^ k) * labels, labels), labels)


def turn():
    rep = lax.axis_index("rep")
    return (rep & 1) * 2 + ((rep >> 1) & 1)


def label_chunk(docs, q, c, lanes, sums):
    qt = q.T
    ct = c.T.astype(F32)
    labels = q.shape[0]

    def products(doc):
        load, enc_ref, enct_ref, gate_ref = doc[:4]
        load()
        enc = enc_ref[...]
        g = gate_ref[:, lanes]
        both = mm(enc, jnp.concatenate([qt, (ct * g).astype(BF16)], axis=1))
        return g, both[:, :labels], both[:, labels:]

    query_grad, class_grad = sums
    ahead = products(docs[0])
    for i, (_, _, enct_ref, gate_ref, attn_ref, score_ref, logit_ref) in enumerate(docs):
        g, scores, attn_grad = ahead
        if i + 1 < len(docs):
            ahead = products(docs[i + 1])
        length = gate_ref[:, gate_ref.shape[1] - LANES :][:, :1]
        token = lax.broadcasted_iota(jnp.int32, scores.shape, 0).astype(F32)
        expo = jnp.where(token < length, jnp.exp(scores), 0.0)
        attn = expo * (1.0 / jnp.sum(expo, axis=0, keepdims=True))
        attn_b = attn.astype(BF16)
        attn_ref[...] = attn_b
        inner = jnp.sum(attn * attn_grad, axis=0, keepdims=True)
        score_grad = (attn * (attn_grad - inner)).astype(BF16)
        score_ref[...] = score_grad
        both = mm(enct_ref[...], jnp.concatenate([attn_b, score_grad], axis=1))
        context, part = both[:, :labels], both[:, labels:]
        query_grad = part if query_grad is None else query_grad + part
        logit_ref[...] = jnp.sum(context * ct, axis=0, keepdims=True)
        part = context * g
        class_grad = part if class_grad is None else class_grad + part
    return query_grad, class_grad


def doc_list(loads, enc_ref, enct_ref, gate_ref, attn_ref, score_ref, logit_ref):
    return [
        (loads[d], enc_ref.at[d], enct_ref.at[d], gate_ref.at[d : d + 1], attn_ref.at[d],
         score_ref.at[d], logit_ref.at[d : d + 1])
        for d in range(enc_ref.shape[0])
    ]


def turn_around(enc_ref, enct_ref, copies=None):
    def load(d):
        if copies is not None:
            copies[d].wait()
        enct_ref[d] = enc_ref[d].T

    return [functools.partial(load, d) for d in range(enc_ref.shape[0])]


def pack_kernel(q_in, c_in, qc_ref, sem):
    copies = [pltpu.make_async_copy(x, qc_ref.at[i], sem.at[i]) for i, x in enumerate((q_in, c_in))]
    for copy in copies:
        copy.start()
    for copy in copies:
        copy.wait()


def make_gates(gate_ref, grad_ref, beam_ref, lens_ref):
    docs, labels = beam_ref.shape
    gate_ref[:, :labels] = grad_ref[...] * beam_ref[...].astype(F32)
    for d in range(docs):
        gate_ref[d : d + 1, labels:] = jnp.full((1, LANES), lens_ref[d], jnp.int32).astype(F32)


def own_kernel(enc_in, beam_in, grad_in, lens_ref, qc_ref, enc_ref, gate_ref, enct_ref,
               attn_ref, score_ref, logit_ref, qsum_ref, csum_ref, beam_ref, grad_ref, sem):
    docs = enc_ref.shape[0]
    small = [(beam_in, beam_ref), (grad_in, grad_ref)]
    small = [pltpu.make_async_copy(x, y, sem.at[docs + i]) for i, (x, y) in enumerate(small)]
    copies = [
        pltpu.make_async_copy(enc_in.at[d], enc_ref.at[d], sem.at[d]) for d in range(docs)
    ]
    for copy in copies[:1] + small + copies[1:]:
        copy.start()
    loads = turn_around(enc_ref, enct_ref, copies)

    def first_load():
        load()
        for copy in small:
            copy.wait()
        make_gates(gate_ref, grad_ref, beam_ref, lens_ref)

    load, loads[0] = loads[0], first_load
    qsum_ref[...], csum_ref[...] = label_chunk(
        doc_list(loads, enc_ref, enct_ref, gate_ref, attn_ref, score_ref, logit_ref),
        qc_ref[0], qc_ref[1], lanes_of(0, qc_ref.shape[1]), (None, None),
    )


def to_blocks(sums, rows_ref, out_refs):
    query_grad, class_grad = sums
    width = query_grad.shape[0]
    rows_ref[:, :width] = query_grad.T
    rows_ref[:, width:] = class_grad.T
    size = rows_ref.shape[0] // GROUP
    count = GROUP // len(out_refs)
    for i in range(GROUP):
        ref = out_refs[i // count]
        block = rows_ref[pl.ds(pl.multiple_of((turn() ^ i) * size, size), size), :]
        ref[(i % count) * size : (i % count + 1) * size, :] = block.astype(ref.dtype)


def other_kernel(lens_ref, beam_ref, grad_ref, enc_ref, qc_ref, qsum_ref, csum_ref,
                 gate_ref, enct_ref, attn_ref, score_ref, logit_ref, *refs):
    make_gates(gate_ref, grad_ref, beam_ref, lens_ref)
    sums = label_chunk(
        doc_list(turn_around(enc_ref, enct_ref), enc_ref, enct_ref, gate_ref,
                 attn_ref, score_ref, logit_ref),
        qc_ref[0], qc_ref[1], lanes_of(0, qc_ref.shape[1]),
        (qsum_ref[...], csum_ref[...]),
    )
    to_blocks(sums, refs[-1], refs[:-1])


def far_kernel(gate_ref, gate2_ref, enc_ref, enc2_ref, enct_ref,
               enct2_ref, qc_ref, attn_ref, score_ref, logit_ref, attn2_ref, score2_ref,
               logit2_ref, *refs):
    loads = [lambda: None] * enc_ref.shape[0]
    sums = label_chunk(
        doc_list(loads, enc_ref, enct_ref, gate_ref, attn_ref, score_ref, logit_ref)
        + doc_list(loads, enc2_ref, enct2_ref, gate2_ref, attn2_ref, score2_ref,
                   logit2_ref),
        qc_ref[0], qc_ref[1], lanes_of(2, qc_ref.shape[1]), (None, None),
    )
    to_blocks(sums, refs[-1], refs[:-1])


def state_parts(ks, gate_ref, chunks):
    docs, labels = gate_ref.shape[0], chunks[2].shape[1]
    ctx_grads = []
    for n, k in enumerate(ks):
        gate = gate_ref[:, lanes_of(k, labels)]
        gate = jnp.concatenate([gate, jnp.zeros((128 - docs, labels), F32)], axis=0).T
        c = chunks[4 * n + 2][1].astype(F32)
        ctx_grads.append([(c * gate[:, d : d + 1]).astype(BF16) for d in range(docs)])
    for d in range(docs):
        total = None
        for n in range(len(ks)):
            attn_ref, score_ref, qc_ref = chunks[4 * n : 4 * n + 3]
            part = mm(attn_ref[d], ctx_grads[n][d]) + mm(score_ref[d], qc_ref[0])
            total = part if total is None else total + part
        yield d, total


def away_kernel(ks, gate_ref, *refs):
    chunks, out_ref = refs[:-1], refs[-1]
    tokens, labels = chunks[0].shape[1:]
    for d, total in state_parts(ks, gate_ref, chunks):
        out_ref[d, :tokens] = total.astype(BF16)
        for n in range(len(ks)):
            logit = chunks[4 * n + 3][d : d + 1, :]
            high = logit.astype(BF16).astype(F32)
            pad = jnp.zeros((EXTRA - 2, labels), F32)
            pair = jnp.concatenate([high, logit - high, pad], axis=0)
            out_ref[d, tokens:, n * labels : (n + 1) * labels] = pair.astype(BF16)


def home_kernel(ks, gate_ref, *refs):
    chunks, (in_ref, out_ref, logit_ref, done_ref, sem) = refs[:-5], refs[-5:]
    tokens, labels = chunks[0].shape[1:]
    copies = []
    for d, total in state_parts(ks, gate_ref, chunks):
        done_ref[d] = (total + in_ref[d, :tokens].astype(F32)).astype(BF16)
        copies.append(pltpu.make_async_copy(done_ref.at[d], out_ref.at[d], sem.at[d]))
        copies[-1].start()
        for n, k in enumerate(ks):
            pair = in_ref[d, tokens:, n * labels : (n + 1) * labels].astype(F32)
            logit_ref[d : d + 1, lanes_of(k, labels)] = chunks[4 * n + 3][d : d + 1, :]
            logit_ref[d : d + 1, lanes_of(k ^ 1, labels)] = pair[0:1] + pair[1:2]
    for copy in copies:
        copy.wait()


def state_grad(gate, parts, more):
    docs, tokens, labels = parts[0][0].shape
    width = parts[0][2].shape[2]
    ins = [gate, *parts[0], *parts[1], *more]
    estimate = cost(4, docs, tokens, width, labels)
    if not more:
        out = shape((docs, tokens + EXTRA, width), BF16)
        return call(functools.partial(away_kernel, (0, 2)), out, ins, "state_away", (), estimate)
    out = shape((docs, tokens, width), BF16)
    return pl.pallas_call(
        functools.partial(home_kernel, (0, 2)),
        out_shape=[out, shape((docs, gate.shape[1] - LANES), F32)],
        in_specs=[VMEM] * len(ins),
        out_specs=[pl.BlockSpec(memory_space=pl.ANY), VMEM],
        scratch_shapes=[pltpu.VMEM(out.shape, BF16), pltpu.SemaphoreType.DMA((docs,))],
        compiler_params=PARAMS,
        cost_estimate=estimate,
        name="state_home",
    )(*ins)


def add_kernel(count, *refs):
    total = refs[0][...].astype(F32)
    for ref in refs[1:count]:
        total = total + ref[...].astype(F32)
    size = refs[count].shape[0]
    for i, ref in enumerate(refs[count:]):
        ref[...] = total[i * size : (i + 1) * size].astype(ref.dtype)


def add(arrays, dtypes, estimate=None):
    rows, cols = arrays[0].shape
    out = [shape((rows // len(dtypes), cols), dtype) for dtype in dtypes]
    return call(
        functools.partial(add_kernel, len(arrays)), out, arrays, "add", estimate=estimate
    )


def rows_kernel(*refs):
    block_refs, (out_ref, rows_ref, sem) = refs[:-3], refs[-3:]
    size = block_refs[0].shape[0]
    copies = []
    for i, ref in enumerate(block_refs):
        rows_ref[i] = ref[...].astype(F32)
        to = pl.ds(pl.multiple_of((turn() ^ i) * size, size), size)
        copies.append(pltpu.make_async_copy(rows_ref.at[i], out_ref.at[to], sem.at[i]))
        copies[-1].start()
    for copy in copies:
        copy.wait()


def to_rows(blocks):
    count = len(blocks)
    rows, cols = blocks[0].shape
    return pl.pallas_call(
        rows_kernel,
        out_shape=shape((count * rows, cols), F32),
        in_specs=[VMEM] * count,
        out_specs=pl.BlockSpec(memory_space=pl.ANY),
        scratch_shapes=[pltpu.VMEM((count, rows, cols), F32), pltpu.SemaphoreType.DMA((count,))],
        compiler_params=PARAMS,
        name="to_rows",
    )(*blocks)


def per_device(reps, blks, encoded, queries, classifiers, lengths, beam, logit_grad):
    labels, width = queries.shape
    docs, tokens, _ = encoded.shape
    total = reps * blks

    def swap(x, mask):
        return lax.ppermute(x, ("rep", "blk"), [(i, i ^ mask) for i in range(total)])

    core, ax = 1, 2
    ay, az, azz = blks, 2 * blks, 4 * blks
    turns = [0, az, ay, ay | az]

    qc = call(
        pack_kernel, shape((2, labels, width), BF16), [queries, classifiers], "pack",
        [pltpu.SemaphoreType.DMA((2,))], hbm=2,
    )
    encoded2, qc = lax.optimization_barrier((encoded, qc))
    far_qc = swap(qc, ax)
    encoded2, beam2, grad2 = swap(encoded2, core), swap(beam, core), swap(logit_grad, core)
    lengths2 = swap(lengths, core)
    lengths = pltpu.with_memory_space_constraint(lengths, pltpu.HBM)

    per_chunk = [
        shape((docs, tokens, labels), BF16),
        shape((docs, tokens, labels), BF16),
        shape((docs, labels), F32),
    ]
    gates = shape((docs, beam.shape[1] + LANES), F32)
    turned = shape((docs, width, tokens), BF16)
    block = shape((labels // GROUP, 2 * width), BF16)
    halves = [shape((labels // 2, 2 * width), dtype) for dtype in (F32, BF16)]
    rows = [pltpu.VMEM((labels, 2 * width), F32)]
    sums = [shape((width, labels), F32)] * 2
    estimate = functools.partial(cost, tokens=tokens, width=width, labels=labels)

    enc, gate, enct, attn, score, logit, *acc = call(
        own_kernel,
        [shape(encoded.shape, BF16), gates, turned] + per_chunk + sums,
        [encoded, beam, logit_grad, lengths, qc], "own_labels",
        [pltpu.VMEM(beam.shape, jnp.int32), pltpu.VMEM(beam.shape, F32),
         pltpu.SemaphoreType.DMA((docs + 2,))],
        estimate(4, docs), hbm=3,
    )
    gate2, enct2, attn2, score2, logit2, keep, send = call(
        other_kernel, [gates, turned] + per_chunk + halves,
        [lengths2, beam2, grad2, encoded2, qc, *acc], "own_labels_other_docs",
        rows, estimate(4, docs),
    )
    received = swap(send, ay)
    far_attn, far_score, far_logit, far_attn2, far_score2, far_logit2, *far = call(
        far_kernel, per_chunk + per_chunk + [shape(block.shape, F32)] + [block] * (GROUP - 1),
        [gate, gate2, enc, encoded2, enct, enct2, far_qc],
        "far_labels", rows, estimate(4, 2 * docs),
    )

    far, keep, received = lax.optimization_barrier((far, keep, received))
    keep, send = add([keep, received], [F32, BF16])
    send, far = lax.optimization_barrier((send, far))
    relayed = swap(far[2], ay)
    received = [swap(far[3], ax | ay | az), swap(far[1], ax | az)]
    (first,) = add([far[0], relayed], [BF16])
    first, send, far_attn2 = lax.optimization_barrier((first, send, far_attn2))
    received.append(swap(first, ax))
    near = swap(send, az)
    state2 = state_grad(
        gate2,
        [(attn2, score2, qc, logit2), (far_attn2, far_score2, far_qc, far_logit2)], [],
    )
    received, near = lax.optimization_barrier((received, near))
    state_in = swap(state2, core)
    (own,) = add([keep, near, *received], [BF16], LONG)
    far_attn, far_score, own = lax.optimization_barrier((far_attn, far_score, own))
    state, logits = state_grad(
        gate, [(attn, score, qc, logit), (far_attn, far_score, far_qc, far_logit)],
        [state_in],
    )
    received, state = lax.optimization_barrier((swap(own, azz), state))
    (own,) = add([own, received], [BF16])
    if reps > 8:
        members = [[i * 8 + j for i in range(reps // 8)] for j in range(8)]
        own = lax.psum(own.astype(F32), "rep", axis_index_groups=members).astype(BF16)

    both, second, first = lax.optimization_barrier([swap(own, mask) for mask in turns[:0:-1]])
    label_grad = to_rows([own, first, second, both])
    return logits, state, label_grad


def solution(mesh):
    reps, blks = mesh.shape["rep"], mesh.shape["blk"]
    assert blks == 4 and reps >= 8 and reps & (reps - 1) == 0
    in_specs = (
        P(("rep", "blk"), None, None),
        P("blk", None),
        P("blk", None),
        P(("rep", "blk")),
        P(("rep", "blk"), None),
        P(("rep", "blk"), None),
    )
    out_specs = (P(("rep", "blk"), None), P(("rep", "blk"), None, None), P("blk", None))
    return jax.shard_map(
        functools.partial(per_device, reps, blks),
        mesh=mesh, in_specs=in_specs, out_specs=out_specs, check_vma=False,
    )
```

profile of v0, /device:TPU:0, one launch (start us, length us, event | category | flops | bytes accessed | tf_op | source)
XLA Modules:
  0.0 56.2 jit_solution(6779085654400672150)
XLA Ops:
  0.6 1.0 %pack.1.qc_ref.refs_2_ = bf16[2,256,512]{2,1,0:T(8,128)(2,1)S(1)} custom-call(bf16[256,512]{1,0:T(8,128)(2,1)} %q_in.1, bf16[256,512]{1,0:T(8,128)(2,1)} %c_in.1), custom_call_target="tpu_custom_call" | custom-call | tf_op jit(solution)/shard_map/pack/pallas_call | solution.py:43
  1.7 0.5 collective-permute-start.3
  2.2 2.6 %collective-permute-start.4 = (bf16[2,256,512]{2,1,0:T(8,128)(2,1)S(1)}, bf16[2,256,512]{2,1,0:T(8,128)(2,1)S(1)}, u32[]{:S(2)}, u32[]{:S(2)}) collective-permute-start(bf16[2,256,512]{2,1,0:T(8,128)(2,1)S(1)} %pack.1.qc_ref.refs_2_), channel_id=1, source_target_pairs={{0,2},{1,3},{2,0},{3,1},{4,6},{5,7},{6,4},{7,5},{8,10},{9,11},{10,... | collective-permute-start | bytes 1572872 | tf_op jit(solution)/shard_map/ppermute | solution.py:315
  4.8 0.2 collective-permute-start
  4.9 0.3 collective-permute-start.1
  5.3 0.2 collective-permute-start.2
  5.4 5.1 %own_labels.1 = (bf16[4,512,512]{2,1,0:T(8,128)(2,1)S(1)}, f32[4,1152]{1,0:T(4,128)S(1)}, bf16[4,512,512]{2,1,0:T(8,128)(2,1)S(1)}, bf16[4,512,256]{2,1,0:T(8,12...) custom-call(bf16[4,512,512]{2,1,0:T(8,128)(2,1)} %enc_in.1, ...), custom_call_target="tpu_custom_call" | custom-call | flops 2147483648 | bytes 4194304 | tf_op jit(solution)/shard_map/own_labels/pallas_call | solution.py:43
  10.6 0.0 collective-permute-done.lens_ref
  10.6 0.0 collective-permute-done.1.beam_ref
  10.6 0.0 collective-permute-done.2.grad_ref
  10.6 0.0 collective-permute-done.3.enc_ref.enc2_ref
  10.6 3.6 %own_labels_other_docs.1 = (f32[4,1152]{1,0:T(4,128)S(1)}, bf16[4,512,512]{2,1,0:T(8,128)(2,1)S(1)}, bf16[4,512,256]{2,1,0:T(8,128)(2,1)S(1)}, bf16[4,512,256]{2...) custom-call(s32[4]{0:T(128)S(1)} %collective-permute-done.lens_ref, ...), custom_call_target="tpu_custom_call" | custom-call | flops 2147483648 | bytes 4194304 | tf_op jit(solution)/shard_map/own_labels_other_docs/pallas_call | solution.py:43
  14.2 1.6 %collective-permute-start.5 = (bf16[128,1024]{1,0:T(8,128)(2,1)S(1)}, bf16[128,1024]{1,0:T(8,128)(2,1)S(1)}, u32[]{:S(2)}, u32[]{:S(2)}) collective-permute-start(bf16[128,1024]{1,0:T(8,128)(2,1)S(1)} %get-tuple-element.79), channel_id=1, source_target_pairs={{0,4},{1,5},{2,6},{3,7},{4,0},{5,1},{6,2},{7,3},{8,12},{9,13},{10,... | collective-permute-start | bytes 786440 | tf_op jit(solution)/shard_map/ppermute | solution.py:315
  15.8 1.5 %collective-permute-done.4.qc_ref.refs_6_ = bf16[2,256,512]{2,1,0:T(8,128)(2,1)S(1)} collective-permute-done((bf16[2,256,512]{2,1,0:T(8,128)(2,1)S(1)}, bf16[2,256,512]{2,1,0:T(8,128)(2,1)S(1)}, u32[]{:S(2)}, u32[]{:S(2)}) %collective-permute-start.4) | collective-permute-done | bytes 524320 | tf_op jit(solution)/shard_map/ppermute | solution.py:315
  17.3 5.5 %far_labels.1 = (bf16[4,512,256]{2,1,0:T(8,128)(2,1)S(1)}, bf16[4,512,256]{2,1,0:T(8,128)(2,1)S(1)}, f32[4,256]{1,0:T(4,128)S(1)}, bf16[4,512,256]{2,1,0:T(8,128...) custom-call(f32[4,1152]{1,0:T(4,128)S(1)} %get-tuple-element.61.gate, ...), custom_call_target="tpu_custom_call" | custom-call | flops 4294967296 | bytes 8388608 | tf_op jit(solution)/shard_map/far_labels/pallas_call | solution.py:43
  22.8 0.0 collective-permute-done.5.refs_1_
  22.9 1.8 %collective-permute-start.8 = (bf16[64,1024]{1,0:T(8,128)(2,1)S(1)}, bf16[64,1024]{1,0:T(8,128)(2,1)S(1)}, u32[]{:S(2)}, u32[]{:S(2)}) collective-permute-start(bf16[64,1024]{1,0:T(8,128)(2,1)S(1)} %get-tuple-element.91), channel_id=1, source_target_pairs={{0,4},{1,5},{2,6},{3,7},{4,0},{5,1},{6,2},{7,3},{8,12},{9,13},{10,... | collective-permute-start | bytes 393224 | tf_op jit(solution)/shard_map/ppermute | solution.py:315
  24.7 2.5 %collective-permute-start.6 = (bf16[64,1024]{1,0:T(8,128)(2,1)S(1)}, bf16[64,1024]{1,0:T(8,128)(2,1)S(1)}, u32[]{:S(2)}, u32[]{:S(2)}) collective-permute-start(bf16[64,1024]{1,0:T(8,128)(2,1)S(1)} %get-tuple-element.88), channel_id=1, source_target_pairs={{0,14},{1,15},{2,12},{3,13},{4,10},{5,11},{6,8},{7,9},{8,6},{9,7},... | collective-permute-start | bytes 393224 | tf_op jit(solution)/shard_map/ppermute | solution.py:315
  27.2 0.2 collective-permute-start.7
  27.4 2.8 %collective-permute-done.8.refs_1_ = bf16[64,1024]{1,0:T(8,128)(2,1)S(1)} collective-permute-done((bf16[64,1024]{1,0:T(8,128)(2,1)S(1)}, bf16[64,1024]{1,0:T(8,128)(2,1)S(1)}, u32[]{:S(2)}, u32[]{:S(2)}) %collective-permute-start.8) | collective-permute-done | bytes 131104 | tf_op jit(solution)/shard_map/ppermute | solution.py:315
  30.2 0.5 collective-permute-start.9
  30.7 1.6 %collective-permute-start.10 = (bf16[64,1024]{1,0:T(8,128)(2,1)S(1)}, bf16[64,1024]{1,0:T(8,128)(2,1)S(1)}, u32[]{:S(2)}, u32[]{:S(2)}) collective-permute-start(bf16[64,1024]{1,0:T(8,128)(2,1)S(1)} %get-tuple-element.95), channel_id=1, source_target_pairs={{0,8},{1,9},{2,10},{3,11},{4,12},{5,13},{6,14},{7,15},{8,0},{9,1},... | collective-permute-start | bytes 393224 | tf_op jit(solution)/shard_map/ppermute | solution.py:315
  32.2 2.7 %state_away.1 = bf16[4,528,512]{2,1,0:T(8,128)(2,1)S(1)} custom-call(f32[4,1152]{1,0:T(4,128)S(1)} %get-tuple-element.68.gate2_ref.gate_ref, bf16[4,512,256]{2,1,0:T(8,128)(2,1)S(1)} %get-tuple-element.103.refs_0_, bf16[4,512,256]{2,1,0:T(8,128)(2,1)S(1)} %get-tuple-element.104.refs_1_, bf16[2,256,512]{2,1,0:T(8,128)(2,1)S(1)} %pack.1.qc_ref.refs_2_, ...), custom_call_target="tpu_custom_call" | custom-call | flops 2147483648 | bytes 4194304 | tf_op jit(solution)/shard_map/state_away/pallas_call | solution.py:43
  34.9 0.1 collective-permute-start.11
  35.0 0.0 collective-permute-done.6.refs_2_
  35.0 0.0 collective-permute-done.7.refs_3_
  35.0 0.9 %collective-permute-done.9.refs_4_ = bf16[64,1024]{1,0:T(8,128)(2,1)S(1)} collective-permute-done((bf16[64,1024]{1,0:T(8,128)(2,1)S(1)}, bf16[64,1024]{1,0:T(8,128)(2,1)S(1)}, u32[]{:S(2)}, u32[]{:S(2)}) %collective-permute-start.9) | collective-permute-done | bytes 131104 | tf_op jit(solution)/shard_map/ppermute | solution.py:315
  36.0 0.1 collective-permute-done.10.refs_1_
  36.1 0.1 add.6.refs_0_
  36.2 2.7 %collective-permute-start.12 = (bf16[64,1024]{1,0:T(8,128)(2,1)S(1)}, bf16[64,1024]{1,0:T(8,128)(2,1)S(1)}, u32[]{:S(2)}, u32[]{:S(2)}) collective-permute-start(bf16[64,1024]{1,0:T(8,128)(2,1)S(1)} %add.6.refs_0_), channel_id=1, source_target_pairs={{0,16},{1,17},{2,18},{3,19},{4,20},{5,21},{6,22},{7,23},{8,24},{9,... | collective-permute-start | bytes 393224 | tf_op jit(solution)/shard_map/ppermute | solution.py:315
  38.9 0.3 collective-permute-done.11.refs_8_
  39.2 4.0 %state_home.1 = (bf16[4,512,512]{2,1,0:T(8,128)(2,1)}, f32[4,1024]{1,0:T(4,128)}) custom-call(f32[4,1152]{1,0:T(4,128)S(1)} %get-tuple-element.61.gate_ref, bf16[4,512,256]{2,1,0:T(8,128)(2,1)S(1)} %get-tuple-element.62.refs_0_, bf16[4,512,256]{2,1,0:T(8,128)(2,1)S(1)} %get-tuple-element.63.refs_1_, bf16[2,256,512]{2,1,0:T(8,128)(2,1)S(1)} %pack.1.qc_ref.refs_2_, ...), custom_call_target="tpu_custom_call" | custom-call | flops 2147483648 | bytes 4194304 | tf_op jit(solution)/shard_map/state_home/pallas_call | solution.py:253
  43.3 1.6 %collective-permute-done.12.refs_1_ = bf16[64,1024]{1,0:T(8,128)(2,1)S(1)} collective-permute-done((bf16[64,1024]{1,0:T(8,128)(2,1)S(1)}, bf16[64,1024]{1,0:T(8,128)(2,1)S(1)}, u32[]{:S(2)}, u32[]{:S(2)}) %collective-permute-start.12) | collective-permute-done | bytes 131104 | tf_op jit(solution)/shard_map/ppermute | solution.py:315
  44.9 0.8 %collective-permute-start.15 = (bf16[64,1024]{1,0:T(8,128)(2,1)S(1)}, bf16[64,1024]{1,0:T(8,128)(2,1)S(1)}, u32[]{:S(2)}, u32[]{:S(2)}) collective-permute-start(bf16[64,1024]{1,0:T(8,128)(2,1)S(1)} %add.7.refs_0_), channel_id=1, source_target_pairs={{0,8},{1,9},{2,10},{3,11},{4,12},{5,13},{6,14},{7,15},{8,0},{9,1},... | collective-permute-start | bytes 393224 | tf_op jit(solution)/shard_map/ppermute | solution.py:315
  45.6 1.8 %collective-permute-start.14 = (bf16[64,1024]{1,0:T(8,128)(2,1)S(1)}, bf16[64,1024]{1,0:T(8,128)(2,1)S(1)}, u32[]{:S(2)}, u32[]{:S(2)}) collective-permute-start(bf16[64,1024]{1,0:T(8,128)(2,1)S(1)} %add.7.refs_0_), channel_id=1, source_target_pairs={{0,4},{1,5},{2,6},{3,7},{4,0},{5,1},{6,2},{7,3},{8,12},{9,13},{10,... | collective-permute-start | bytes 393224 | tf_op jit(solution)/shard_map/ppermute | solution.py:315
  47.5 1.4 %collective-permute-start.13 = (bf16[64,1024]{1,0:T(8,128)(2,1)S(1)}, bf16[64,1024]{1,0:T(8,128)(2,1)S(1)}, u32[]{:S(2)}, u32[]{:S(2)}) collective-permute-start(bf16[64,1024]{1,0:T(8,128)(2,1)S(1)} %add.7.refs_0_), channel_id=1, source_target_pairs={{0,12},{1,13},{2,14},{3,15},{4,8},{5,9},{6,10},{7,11},{8,4},{9,5},... | collective-permute-start | bytes 393224 | tf_op jit(solution)/shard_map/ppermute | solution.py:315
  48.8 1.2 %collective-permute-done.15.refs_1_ = bf16[64,1024]{1,0:T(8,128)(2,1)S(1)} collective-permute-done((bf16[64,1024]{1,0:T(8,128)(2,1)S(1)}, bf16[64,1024]{1,0:T(8,128)(2,1)S(1)}, u32[]{:S(2)}, u32[]{:S(2)}) %collective-permute-start.15) | collective-permute-done | bytes 131104 | tf_op jit(solution)/shard_map/ppermute | solution.py:315
  50.1 3.1 %collective-permute-done.14.refs_2_ = bf16[64,1024]{1,0:T(8,128)(2,1)S(1)} collective-permute-done((bf16[64,1024]{1,0:T(8,128)(2,1)S(1)}, bf16[64,1024]{1,0:T(8,128)(2,1)S(1)}, u32[]{:S(2)}, u32[]{:S(2)}) %collective-permute-start.14) | collective-permute-done | bytes 131104 | tf_op jit(solution)/shard_map/ppermute | solution.py:315
  53.2 1.8 %collective-permute-done.13.refs_3_ = bf16[64,1024]{1,0:T(8,128)(2,1)S(1)} collective-permute-done((bf16[64,1024]{1,0:T(8,128)(2,1)S(1)}, bf16[64,1024]{1,0:T(8,128)(2,1)S(1)}, u32[]{:S(2)}, u32[]{:S(2)}) %collective-permute-start.13) | collective-permute-done | bytes 131104 | tf_op jit(solution)/shard_map/ppermute | solution.py:315
  55.0 1.0 %to_rows.1 = f32[256,1024]{1,0:T(8,128)} custom-call(bf16[64,1024]{1,0:T(8,128)(2,1)S(1)} %add.7.refs_0_, bf16[64,1024]{1,0:T(8,128)(2,1)S(1)} %collective-permute-done.15.refs_1_, bf16[64,1024]{1,0:T(8,128)(2,1)S(1)} %collective-permute-done.14.refs_2_, bf16[64,1024]{1,0:T(8,128)(2,1)S(1)} %collective-permute-done.13.refs_3_), custom_call_target="tpu_custom_call" | custom-call | tf_op jit(solution)/shard_map/to_rows/pallas_call | solution.py:298
  (3 shorter events, 0.1 us)
Async XLA Ops:
  1.7 8.9 %collective-permute-start.3 = (bf16[4,512,512]{2,1,0:T(8,128)(2,1)}, bf16[4,512,512]{2,1,0:T(8,128)(2,1)S(1)}, u32[]{:S(2)}, u32[]{:S(2)}) collective-permute-start(bf16[4,512,512]{2,1,0:T(8,128)(2,1)} %enc_in.1), channel_id=1, source_target_pairs={{0,1},{1,0},{2,3},{3,2},{4,5},{5,4},{6,7},{7,6},{8,9},{9,8},{10,11... | collective-permute-start | bytes 6291464 | tf_op jit(solution)/shard_map/ppermute | solution.py:315
  2.2 15.1 %collective-permute-start.4 = (bf16[2,256,512]{2,1,0:T(8,128)(2,1)S(1)}, bf16[2,256,512]{2,1,0:T(8,128)(2,1)S(1)}, u32[]{:S(2)}, u32[]{:S(2)}) collective-permute-start(bf16[2,256,512]{2,1,0:T(8,128)(2,1)S(1)} %pack.1.qc_ref.refs_2_), channel_id=1, source_target_pairs={{0,2},{1,3},{2,0},{3,1},{4,6},{5,7},{6,4},{7,5},{8,10},{9,11},{10,... | collective-permute-start | bytes 1572872 | tf_op jit(solution)/shard_map/ppermute | solution.py:315
  4.8 5.8 %collective-permute-start = (s32[4]{0:T(128)}, s32[4]{0:T(128)S(1)}, u32[]{:S(2)}, u32[]{:S(2)}) collective-permute-start(s32[4]{0:T(128)} %lens_ref.1), channel_id=1, source_target_pairs={{0,1},{1,0},{2,3},{3,2},{4,5},{5,4},{6,7},{7,6},{8,9},{9,8},{10,11... | collective-permute-start | bytes 56 | tf_op jit(solution)/shard_map/ppermute | solution.py:315
  4.9 5.6 %collective-permute-start.1 = (s32[4,1024]{1,0:T(4,128)}, s32[4,1024]{1,0:T(4,128)S(1)}, u32[]{:S(2)}, u32[]{:S(2)}) collective-permute-start(s32[4,1024]{1,0:T(4,128)} %beam_in.1), channel_id=1, source_target_pairs={{0,1},{1,0},{2,3},{3,2},{4,5},{5,4},{6,7},{7,6},{8,9},{9,8},{10,11... | collective-permute-start | bytes 49160 | tf_op jit(solution)/shard_map/ppermute | solution.py:315
  5.3 5.3 %collective-permute-start.2 = (f32[4,1024]{1,0:T(4,128)}, f32[4,1024]{1,0:T(4,128)S(1)}, u32[]{:S(2)}, u32[]{:S(2)}) collective-permute-start(f32[4,1024]{1,0:T(4,128)} %grad_in.1), channel_id=1, source_target_pairs={{0,1},{1,0},{2,3},{3,2},{4,5},{5,4},{6,7},{7,6},{8,9},{9,8},{10,11... | collective-permute-start | bytes 49160 | tf_op jit(solution)/shard_map/ppermute | solution.py:315
  14.2 8.6 %collective-permute-start.5 = (bf16[128,1024]{1,0:T(8,128)(2,1)S(1)}, bf16[128,1024]{1,0:T(8,128)(2,1)S(1)}, u32[]{:S(2)}, u32[]{:S(2)}) collective-permute-start(bf16[128,1024]{1,0:T(8,128)(2,1)S(1)} %get-tuple-element.79), channel_id=1, source_target_pairs={{0,4},{1,5},{2,6},{3,7},{4,0},{5,1},{6,2},{7,3},{8,12},{9,13},{10,... | collective-permute-start | bytes 786440 | tf_op jit(solution)/shard_map/ppermute | solution.py:315
  22.9 7.2 %collective-permute-start.8 = (bf16[64,1024]{1,0:T(8,128)(2,1)S(1)}, bf16[64,1024]{1,0:T(8,128)(2,1)S(1)}, u32[]{:S(2)}, u32[]{:S(2)}) collective-permute-start(bf16[64,1024]{1,0:T(8,128)(2,1)S(1)} %get-tuple-element.91), channel_id=1, source_target_pairs={{0,4},{1,5},{2,6},{3,7},{4,0},{5,1},{6,2},{7,3},{8,12},{9,13},{10,... | collective-permute-start | bytes 393224 | tf_op jit(solution)/shard_map/ppermute | solution.py:315
  24.7 10.3 %collective-permute-start.6 = (bf16[64,1024]{1,0:T(8,128)(2,1)S(1)}, bf16[64,1024]{1,0:T(8,128)(2,1)S(1)}, u32[]{:S(2)}, u32[]{:S(2)}) collective-permute-start(bf16[64,1024]{1,0:T(8,128)(2,1)S(1)} %get-tuple-element.88), channel_id=1, source_target_pairs={{0,14},{1,15},{2,12},{3,13},{4,10},{5,11},{6,8},{7,9},{8,6},{9,7},... | collective-permute-start | bytes 393224 | tf_op jit(solution)/shard_map/ppermute | solution.py:315
  27.2 7.8 %collective-permute-start.7 = (bf16[64,1024]{1,0:T(8,128)(2,1)S(1)}, bf16[64,1024]{1,0:T(8,128)(2,1)S(1)}, u32[]{:S(2)}, u32[]{:S(2)}) collective-permute-start(bf16[64,1024]{1,0:T(8,128)(2,1)S(1)} %get-tuple-element.89), channel_id=1, source_target_pairs={{0,10},{1,11},{2,8},{3,9},{4,14},{5,15},{6,12},{7,13},{8,2},{9,3},... | collective-permute-start | bytes 393224 | tf_op jit(solution)/shard_map/ppermute | solution.py:315
  30.2 5.8 %collective-permute-start.9 = (bf16[64,1024]{1,0:T(8,128)(2,1)S(1)}, bf16[64,1024]{1,0:T(8,128)(2,1)S(1)}, u32[]{:S(2)}, u32[]{:S(2)}) collective-permute-start(bf16[64,1024]{1,0:T(8,128)(2,1)S(1)} %add.5), channel_id=1, source_target_pairs={{0,2},{1,3},{2,0},{3,1},{4,6},{5,7},{6,4},{7,5},{8,10},{9,11},{10,... | collective-permute-start | bytes 393224 | tf_op jit(solution)/shard_map/ppermute | solution.py:315
  30.7 5.4 %collective-permute-start.10 = (bf16[64,1024]{1,0:T(8,128)(2,1)S(1)}, bf16[64,1024]{1,0:T(8,128)(2,1)S(1)}, u32[]{:S(2)}, u32[]{:S(2)}) collective-permute-start(bf16[64,1024]{1,0:T(8,128)(2,1)S(1)} %get-tuple-element.95), channel_id=1, source_target_pairs={{0,8},{1,9},{2,10},{3,11},{4,12},{5,13},{6,14},{7,15},{8,0},{9,1},... | collective-permute-start | bytes 393224 | tf_op jit(solution)/shard_map/ppermute | solution.py:315
  34.9 4.3 %collective-permute-start.11 = (bf16[4,528,512]{2,1,0:T(8,128)(2,1)S(1)}, bf16[4,528,512]{2,1,0:T(8,128)(2,1)S(1)}, u32[]{:S(2)}, u32[]{:S(2)}) collective-permute-start(bf16[4,528,512]{2,1,0:T(8,128)(2,1)S(1)} %state_away.1), channel_id=1, source_target_pairs={{0,1},{1,0},{2,3},{3,2},{4,5},{5,4},{6,7},{7,6},{8,9},{9,8},{10,11... | collective-permute-start | bytes 6488072 | tf_op jit(solution)/shard_map/ppermute | solution.py:315
  36.2 8.7 %collective-permute-start.12 = (bf16[64,1024]{1,0:T(8,128)(2,1)S(1)}, bf16[64,1024]{1,0:T(8,128)(2,1)S(1)}, u32[]{:S(2)}, u32[]{:S(2)}) collective-permute-start(bf16[64,1024]{1,0:T(8,128)(2,1)S(1)} %add.6.refs_0_), channel_id=1, source_target_pairs={{0,16},{1,17},{2,18},{3,19},{4,20},{5,21},{6,22},{7,23},{8,24},{9,... | collective-permute-start | bytes 393224 | tf_op jit(solution)/shard_map/ppermute | solution.py:315
  44.9 5.2 %collective-permute-start.15 = (bf16[64,1024]{1,0:T(8,128)(2,1)S(1)}, bf16[64,1024]{1,0:T(8,128)(2,1)S(1)}, u32[]{:S(2)}, u32[]{:S(2)}) collective-permute-start(bf16[64,1024]{1,0:T(8,128)(2,1)S(1)} %add.7.refs_0_), channel_id=1, source_target_pairs={{0,8},{1,9},{2,10},{3,11},{4,12},{5,13},{6,14},{7,15},{8,0},{9,1},... | collective-permute-start | bytes 393224 | tf_op jit(solution)/shard_map/ppermute | solution.py:315
  45.6 7.6 %collective-permute-start.14 = (bf16[64,1024]{1,0:T(8,128)(2,1)S(1)}, bf16[64,1024]{1,0:T(8,128)(2,1)S(1)}, u32[]{:S(2)}, u32[]{:S(2)}) collective-permute-start(bf16[64,1024]{1,0:T(8,128)(2,1)S(1)} %add.7.refs_0_), channel_id=1, source_target_pairs={{0,4},{1,5},{2,6},{3,7},{4,0},{5,1},{6,2},{7,3},{8,12},{9,13},{10,... | collective-permute-start | bytes 393224 | tf_op jit(solution)/shard_map/ppermute | solution.py:315
  47.5 7.6 %collective-permute-start.13 = (bf16[64,1024]{1,0:T(8,128)(2,1)S(1)}, bf16[64,1024]{1,0:T(8,128)(2,1)S(1)}, u32[]{:S(2)}, u32[]{:S(2)}) collective-permute-start(bf16[64,1024]{1,0:T(8,128)(2,1)S(1)} %add.7.refs_0_), channel_id=1, source_target_pairs={{0,12},{1,13},{2,14},{3,15},{4,8},{5,9},{6,10},{7,11},{8,4},{9,5},... | collective-permute-start | bytes 393224 | tf_op jit(solution)/shard_map/ppermute | solution.py:315
where the time goes:
time: 56.4 us; the launch traced here: 56.2 us
  Pallas kernels  23.2 us (41%)
  starting transfers between devices  18.7 us (33%)
  waiting for transfers between devices  13.5 us (24%)
  between operations  0.92 us (2%)
    ppermute x16, starting transfers between devices, swap(): lax.ppermute(x, ('rep', 'blk'), [(i, i ^ mask) for i in range(total)])  18.7 us
    pallas_call x9, Pallas kernels, call(): pl.pallas_call(kernel, out_shape=out_shape, in_specs=[HBM if i < hbm else...  18.2 us
    ppermute x16, waiting for transfers between devices, swap(): lax.ppermute(x, ('rep', 'blk'), [(i, i ^ mask) for i in range(total)])  13.5 us
    pallas_call x1, Pallas kernels, state_grad(): pl.pallas_call(functools.partial(home_kernel, (0, 2)), out_shape=[out, sh...  4 us
  transfers between devices with their start and end apart: 16, of which 9 were waited for; matrix products, arithmetic and copies ran while one was open for 0% of the time, Pallas kernels for 37%

commit v1 on v0

--- a/solution.py
+++ b/solution.py
@@ -125,6 +125,16 @@
         copy.wait()
 
 
+def after_first(loads, then):
+    load = loads[0]
+
+    def both():
+        load()
+        then()
+
+    loads[0] = both
+
+
 def make_gates(gate_ref, grad_ref, beam_ref, lens_ref):
     docs, labels = beam_ref.shape
     gate_ref[:, :labels] = grad_ref[...] * beam_ref[...].astype(F32)
@@ -132,10 +142,10 @@
         gate_ref[d : d + 1, labels:] = jnp.full((1, LANES), lens_ref[d], jnp.int32).astype(F32)
 
 
-def own_kernel(enc_in, beam_in, grad_in, lens_ref, qc_ref, enc_ref, gate_ref, enct_ref,
-               attn_ref, score_ref, logit_ref, qsum_ref, csum_ref, beam_ref, grad_ref, sem):
+def own_kernel(enc_in, beam_in, grad_in, lens_in, qc_ref, enc_ref, gate_ref, enct_ref, attn_ref,
+               score_ref, logit_ref, qsum_ref, csum_ref, beam_ref, grad_ref, lens_ref, sem):
     docs = enc_ref.shape[0]
-    small = [(beam_in, beam_ref), (grad_in, grad_ref)]
+    small = [(beam_in, beam_ref), (grad_in, grad_ref), (lens_in, lens_ref)]
     small = [pltpu.make_async_copy(x, y, sem.at[docs + i]) for i, (x, y) in enumerate(small)]
     copies = [
         pltpu.make_async_copy(enc_in.at[d], enc_ref.at[d], sem.at[d]) for d in range(docs)
@@ -144,13 +154,12 @@
         copy.start()
     loads = turn_around(enc_ref, enct_ref, copies)
 
-    def first_load():
-        load()
+    def gates():
         for copy in small:
             copy.wait()
         make_gates(gate_ref, grad_ref, beam_ref, lens_ref)
 
-    load, loads[0] = loads[0], first_load
+    after_first(loads, gates)
     qsum_ref[...], csum_ref[...] = label_chunk(
         doc_list(loads, enc_ref, enct_ref, gate_ref, attn_ref, score_ref, logit_ref),
         qc_ref[0], qc_ref[1], lanes_of(0, qc_ref.shape[1]), (None, None),
@@ -170,14 +179,21 @@
         ref[(i % count) * size : (i % count + 1) * size, :] = block.astype(ref.dtype)
 
 
-def other_kernel(lens_ref, beam_ref, grad_ref, enc_ref, qc_ref, qsum_ref, csum_ref,
-                 gate_ref, enct_ref, attn_ref, score_ref, logit_ref, *refs):
-    make_gates(gate_ref, grad_ref, beam_ref, lens_ref)
+def other_kernel(lens_in, beam_ref, grad_ref, enc_ref, qc_ref, qsum_ref, csum_ref, gate_ref,
+                 enct_ref, attn_ref, score_ref, logit_ref, *refs):
+    refs, (lens_ref, sem) = refs[:-2], refs[-2:]
+    copy = pltpu.make_async_copy(lens_in, lens_ref, sem)
+    copy.start()
+
+    def gates():
+        copy.wait()
+        make_gates(gate_ref, grad_ref, beam_ref, lens_ref)
+
+    loads = turn_around(enc_ref, enct_ref)
+    after_first(loads, gates)
     sums = label_chunk(
-        doc_list(turn_around(enc_ref, enct_ref), enc_ref, enct_ref, gate_ref,
-                 attn_ref, score_ref, logit_ref),
-        qc_ref[0], qc_ref[1], lanes_of(0, qc_ref.shape[1]),
-        (qsum_ref[...], csum_ref[...]),
+        doc_list(loads, enc_ref, enct_ref, gate_ref, attn_ref, score_ref, logit_ref),
+        qc_ref[0], qc_ref[1], lanes_of(0, qc_ref.shape[1]), (qsum_ref[...], csum_ref[...]),
     )
     to_blocks(sums, refs[-1], refs[:-1])
 
@@ -326,7 +342,6 @@
     far_qc = swap(qc, ax)
     encoded2, beam2, grad2 = swap(encoded2, core), swap(beam, core), swap(logit_grad, core)
     lengths2 = swap(lengths, core)
-    lengths = pltpu.with_memory_space_constraint(lengths, pltpu.HBM)
 
     per_chunk = [
         shape((docs, tokens, labels), BF16),
@@ -346,13 +361,14 @@
         [shape(encoded.shape, BF16), gates, turned] + per_chunk + sums,
         [encoded, beam, logit_grad, lengths, qc], "own_labels",
         [pltpu.VMEM(beam.shape, jnp.int32), pltpu.VMEM(beam.shape, F32),
-         pltpu.SemaphoreType.DMA((docs + 2,))],
-        estimate(4, docs), hbm=3,
+         pltpu.SMEM((docs,), jnp.int32), pltpu.SemaphoreType.DMA((docs + 3,))],
+        estimate(4, docs), hbm=4,
     )
     gate2, enct2, attn2, score2, logit2, keep, send = call(
         other_kernel, [gates, turned] + per_chunk + halves,
         [lengths2, beam2, grad2, encoded2, qc, *acc], "own_labels_other_docs",
-        rows, estimate(4, docs),
+        rows + [pltpu.SMEM((docs,), jnp.int32), pltpu.SemaphoreType.DMA(())],
+        estimate(4, docs), hbm=1,
     )
     received = swap(send, ay)
     far_attn, far_score, far_logit, far_attn2, far_score2, far_logit2, *far = call(
@@ -365,7 +381,7 @@
     keep, send = add([keep, received], [F32, BF16])
     send, far = lax.optimization_barrier((send, far))
     relayed = swap(far[2], ay)
-    received = [swap(far[3], ax | ay | az), swap(far[1], ax | az)]
+    received = [swap(far[1], ax | az), swap(far[3], ax | ay | az)]
     (first,) = add([far[0], relayed], [BF16])
     first, send, far_attn2 = lax.optimization_barrier((first, send, far_attn2))
     received.append(swap(first, ax))

time: 56.4 us -> 55.3 us (0.980)
  waiting for transfers between devices: 13.5 us -> 11.9 us
  Pallas kernels: 23.2 us -> 22.5 us
  starting transfers between devices: 18.7 us -> 19.3 us
    ppermute x16, waiting for transfers between devices: 13.5 us -> 11.9 us  [swap(): lax.ppermute(x, ('rep', 'blk'), [(i, i ^ mask) for i in range(total)])]
    pallas_call x9, Pallas kernels: 18.2 us -> 17.5 us  [call(): pl.pallas_call(kernel, out_shape=out_shape, in_specs=[HBM if i < hbm else...]
    ppermute x16, starting transfers between devices: 18.7 us -> 19.3 us  [swap(): lax.ppermute(x, ('rep', 'blk'), [(i, i ^ mask) for i in range(total)])]
  transfers between devices with their start and end apart: 16 -> 16, of which waited for: 9 -> 7; matrix products, arithmetic and copies ran while one was open for 0% -> 0% of each run, Pallas kernels for 37% -> 37%
where the time goes in v1:
time: 55.3 us; the launch traced here: 55.1 us
  Pallas kernels  22.5 us (41%)
  starting transfers between devices  19.3 us (35%)
  waiting for transfers between devices  11.9 us (22%)
  between operations  0.92 us (2%)
    ppermute x16, starting transfers between devices, swap(): lax.ppermute(x, ('rep', 'blk'), [(i, i ^ mask) for i in range(total)])  19.3 us
    pallas_call x9, Pallas kernels, call(): pl.pallas_call(kernel, out_shape=out_shape, in_specs=[HBM if i < hbm else...  17.5 us
    ppermute x16, waiting for transfers between devices, swap(): lax.ppermute(x, ('rep', 'blk'), [(i, i ^ mask) for i in range(total)])  11.9 us
    pallas_call x1, Pallas kernels, state_grad(): pl.pallas_call(functools.partial(home_kernel, (0, 2)), out_shape=[out, sh...  3.99 us
  transfers between devices with their start and end apart: 16, of which 7 were waited for; matrix products, arithmetic and copies ran while one was open for 0% of the time, Pallas kernels for 37%

profile of v1, /device:TPU:0, one launch (start us, length us, event | category | flops | bytes accessed | tf_op | source)
XLA Modules:
  0.0 55.1 jit_solution(8608403512104522554)
XLA Ops:
  0.6 1.0 %pack.1.qc_ref.refs_2_ = bf16[2,256,512]{2,1,0:T(8,128)(2,1)S(1)} custom-call(bf16[256,512]{1,0:T(8,128)(2,1)} %q_in.1, bf16[256,512]{1,0:T(8,128)(2,1)} %c_in.1), custom_call_target="tpu_custom_call" | custom-call | tf_op jit(solution)/shard_map/pack/pallas_call | solution.py:43
  1.7 0.5 collective-permute-start.3
  2.2 2.6 %collective-permute-start.4 = (bf16[2,256,512]{2,1,0:T(8,128)(2,1)S(1)}, bf16[2,256,512]{2,1,0:T(8,128)(2,1)S(1)}, u32[]{:S(2)}, u32[]{:S(2)}) collective-permute-start(bf16[2,256,512]{2,1,0:T(8,128)(2,1)S(1)} %pack.1.qc_ref.refs_2_), channel_id=1, source_target_pairs={{0,2},{1,3},{2,0},{3,1},{4,6},{5,7},{6,4},{7,5},{8,10},{9,11},{10,... | collective-permute-start | bytes 1572872 | tf_op jit(solution)/shard_map/ppermute | solution.py:331
  4.8 0.2 collective-permute-start
  4.9 0.3 collective-permute-start.1
  5.3 0.2 collective-permute-start.2
  5.4 4.5 %own_labels.1 = (bf16[4,512,512]{2,1,0:T(8,128)(2,1)S(1)}, f32[4,1152]{1,0:T(4,128)S(1)}, bf16[4,512,512]{2,1,0:T(8,128)(2,1)S(1)}, bf16[4,512,256]{2,1,0:T(8,12...) custom-call(bf16[4,512,512]{2,1,0:T(8,128)(2,1)} %enc_in.1, ...), custom_call_target="tpu_custom_call" | custom-call | flops 2147483648 | bytes 4194304 | tf_op jit(solution)/shard_map/own_labels/pallas_call | solution.py:43
  9.9 0.0 collective-permute-done.lens_in
  9.9 0.0 copy-start
  10.0 0.0 collective-permute-done.1.beam_ref
  10.0 0.0 collective-permute-done.2.grad_ref
  10.0 0.0 collective-permute-done.3.enc_ref.enc2_ref
  10.0 0.5 copy-done
  10.5 3.7 %own_labels_other_docs.1 = (f32[4,1152]{1,0:T(4,128)S(1)}, bf16[4,512,512]{2,1,0:T(8,128)(2,1)S(1)}, bf16[4,512,256]{2,1,0:T(8,128)(2,1)S(1)}, bf16[4,512,256]{2...) custom-call(s32[4]{0:T(128)} %copy-done, ...), custom_call_target="tpu_custom_call" | custom-call | flops 2147483648 | bytes 4194304 | tf_op jit(solution)/shard_map/own_labels_other_docs/pallas_call | solution.py:43
  14.2 1.6 %collective-permute-start.5 = (bf16[128,1024]{1,0:T(8,128)(2,1)S(1)}, bf16[128,1024]{1,0:T(8,128)(2,1)S(1)}, u32[]{:S(2)}, u32[]{:S(2)}) collective-permute-start(bf16[128,1024]{1,0:T(8,128)(2,1)S(1)} %get-tuple-element.79), channel_id=1, source_target_pairs={{0,4},{1,5},{2,6},{3,7},{4,0},{5,1},{6,2},{7,3},{8,12},{9,13},{10,... | collective-permute-start | bytes 786440 | tf_op jit(solution)/shard_map/ppermute | solution.py:331
  15.8 1.5 %collective-permute-done.4.qc_ref.refs_6_ = bf16[2,256,512]{2,1,0:T(8,128)(2,1)S(1)} collective-permute-done((bf16[2,256,512]{2,1,0:T(8,128)(2,1)S(1)}, bf16[2,256,512]{2,1,0:T(8,128)(2,1)S(1)}, u32[]{:S(2)}, u32[]{:S(2)}) %collective-permute-start.4) | collective-permute-done | bytes 524320 | tf_op jit(solution)/shard_map/ppermute | solution.py:331
  17.3 5.5 %far_labels.1 = (bf16[4,512,256]{2,1,0:T(8,128)(2,1)S(1)}, bf16[4,512,256]{2,1,0:T(8,128)(2,1)S(1)}, f32[4,256]{1,0:T(4,128)S(1)}, bf16[4,512,256]{2,1,0:T(8,128...) custom-call(f32[4,1152]{1,0:T(4,128)S(1)} %get-tuple-element.61.gate, ...), custom_call_target="tpu_custom_call" | custom-call | flops 4294967296 | bytes 8388608 | tf_op jit(solution)/shard_map/far_labels/pallas_call | solution.py:43
  22.8 0.0 collective-permute-done.5.refs_1_
  22.9 1.8 %collective-permute-start.8 = (bf16[64,1024]{1,0:T(8,128)(2,1)S(1)}, bf16[64,1024]{1,0:T(8,128)(2,1)S(1)}, u32[]{:S(2)}, u32[]{:S(2)}) collective-permute-start(bf16[64,1024]{1,0:T(8,128)(2,1)S(1)} %get-tuple-element.91), channel_id=1, source_target_pairs={{0,4},{1,5},{2,6},{3,7},{4,0},{5,1},{6,2},{7,3},{8,12},{9,13},{10,... | collective-permute-start | bytes 393224 | tf_op jit(solution)/shard_map/ppermute | solution.py:331
  24.7 2.5 %collective-permute-start.6 = (bf16[64,1024]{1,0:T(8,128)(2,1)S(1)}, bf16[64,1024]{1,0:T(8,128)(2,1)S(1)}, u32[]{:S(2)}, u32[]{:S(2)}) collective-permute-start(bf16[64,1024]{1,0:T(8,128)(2,1)S(1)} %get-tuple-element.88), channel_id=1, source_target_pairs={{0,10},{1,11},{2,8},{3,9},{4,14},{5,15},{6,12},{7,13},{8,2},{9,3},... | collective-permute-start | bytes 393224 | tf_op jit(solution)/shard_map/ppermute | solution.py:331
  27.3 0.1 collective-permute-start.7
  27.3 0.8 %collective-permute-done.8.refs_1_ = bf16[64,1024]{1,0:T(8,128)(2,1)S(1)} collective-permute-done((bf16[64,1024]{1,0:T(8,128)(2,1)S(1)}, bf16[64,1024]{1,0:T(8,128)(2,1)S(1)}, u32[]{:S(2)}, u32[]{:S(2)}) %collective-permute-start.8) | collective-permute-done | bytes 131104 | tf_op jit(solution)/shard_map/ppermute | solution.py:331
  28.2 1.6 %collective-permute-start.9 = (bf16[64,1024]{1,0:T(8,128)(2,1)S(1)}, bf16[64,1024]{1,0:T(8,128)(2,1)S(1)}, u32[]{:S(2)}, u32[]{:S(2)}) collective-permute-start(bf16[64,1024]{1,0:T(8,128)(2,1)S(1)} %add.5), channel_id=1, source_target_pairs={{0,2},{1,3},{2,0},{3,1},{4,6},{5,7},{6,4},{7,5},{8,10},{9,11},{10,... | collective-permute-start | bytes 393224 | tf_op jit(solution)/shard_map/ppermute | solution.py:331
  29.9 1.6 %collective-permute-start.10 = (bf16[64,1024]{1,0:T(8,128)(2,1)S(1)}, bf16[64,1024]{1,0:T(8,128)(2,1)S(1)}, u32[]{:S(2)}, u32[]{:S(2)}) collective-permute-start(bf16[64,1024]{1,0:T(8,128)(2,1)S(1)} %get-tuple-element.95), channel_id=1, source_target_pairs={{0,8},{1,9},{2,10},{3,11},{4,12},{5,13},{6,14},{7,15},{8,0},{9,1},... | collective-permute-start | bytes 393224 | tf_op jit(solution)/shard_map/ppermute | solution.py:331
  31.5 2.5 %state_away.1 = bf16[4,528,512]{2,1,0:T(8,128)(2,1)S(1)} custom-call(f32[4,1152]{1,0:T(4,128)S(1)} %get-tuple-element.68.gate2_ref.gate_ref, bf16[4,512,256]{2,1,0:T(8,128)(2,1)S(1)} %get-tuple-element.103.refs_0_, bf16[4,512,256]{2,1,0:T(8,128)(2,1)S(1)} %get-tuple-element.104.refs_1_, bf16[2,256,512]{2,1,0:T(8,128)(2,1)S(1)} %pack.1.qc_ref.refs_2_, ...), custom_call_target="tpu_custom_call" | custom-call | flops 2147483648 | bytes 4194304 | tf_op jit(solution)/shard_map/state_away/pallas_call | solution.py:43
  34.0 0.1 collective-permute-start.11
  34.1 0.0 collective-permute-done.6.refs_2_
  34.1 1.0 %collective-permute-done.7.refs_3_ = bf16[64,1024]{1,0:T(8,128)(2,1)S(1)} collective-permute-done((bf16[64,1024]{1,0:T(8,128)(2,1)S(1)}, bf16[64,1024]{1,0:T(8,128)(2,1)S(1)}, u32[]{:S(2)}, u32[]{:S(2)}) %collective-permute-start.7) | collective-permute-done | bytes 131104 | tf_op jit(solution)/shard_map/ppermute | solution.py:331
  35.1 1.2 %collective-permute-done.9.refs_4_ = bf16[64,1024]{1,0:T(8,128)(2,1)S(1)} collective-permute-done((bf16[64,1024]{1,0:T(8,128)(2,1)S(1)}, bf16[64,1024]{1,0:T(8,128)(2,1)S(1)}, u32[]{:S(2)}, u32[]{:S(2)}) %collective-permute-start.9) | collective-permute-done | bytes 131104 | tf_op jit(solution)/shard_map/ppermute | solution.py:331
  36.2 0.0 collective-permute-done.10.refs_1_
  36.2 0.1 add.6.refs_0_
  36.3 2.7 %collective-permute-start.12 = (bf16[64,1024]{1,0:T(8,128)(2,1)S(1)}, bf16[64,1024]{1,0:T(8,128)(2,1)S(1)}, u32[]{:S(2)}, u32[]{:S(2)}) collective-permute-start(bf16[64,1024]{1,0:T(8,128)(2,1)S(1)} %add.6.refs_0_), channel_id=1, source_target_pairs={{0,16},{1,17},{2,18},{3,19},{4,20},{5,21},{6,22},{7,23},{8,24},{9,... | collective-permute-start | bytes 393224 | tf_op jit(solution)/shard_map/ppermute | solution.py:331
  39.0 0.0 collective-permute-done.11.refs_8_
  39.0 4.0 %state_home.1 = (bf16[4,512,512]{2,1,0:T(8,128)(2,1)}, f32[4,1024]{1,0:T(4,128)}) custom-call(f32[4,1152]{1,0:T(4,128)S(1)} %get-tuple-element.61.gate_ref, bf16[4,512,256]{2,1,0:T(8,128)(2,1)S(1)} %get-tuple-element.62.refs_0_, bf16[4,512,256]{2,1,0:T(8,128)(2,1)S(1)} %get-tuple-element.63.refs_1_, bf16[2,256,512]{2,1,0:T(8,128)(2,1)S(1)} %pack.1.qc_ref.refs_2_, ...), custom_call_target="tpu_custom_call" | custom-call | flops 2147483648 | bytes 4194304 | tf_op jit(solution)/shard_map/state_home/pallas_call | solution.py:269
  43.0 2.5 %collective-permute-done.12.refs_1_ = bf16[64,1024]{1,0:T(8,128)(2,1)S(1)} collective-permute-done((bf16[64,1024]{1,0:T(8,128)(2,1)S(1)}, bf16[64,1024]{1,0:T(8,128)(2,1)S(1)}, u32[]{:S(2)}, u32[]{:S(2)}) %collective-permute-start.12) | collective-permute-done | bytes 131104 | tf_op jit(solution)/shard_map/ppermute | solution.py:331
  45.5 0.6 %collective-permute-start.15 = (bf16[64,1024]{1,0:T(8,128)(2,1)S(1)}, bf16[64,1024]{1,0:T(8,128)(2,1)S(1)}, u32[]{:S(2)}, u32[]{:S(2)}) collective-permute-start(bf16[64,1024]{1,0:T(8,128)(2,1)S(1)} %add.7.refs_0_), channel_id=1, source_target_pairs={{0,8},{1,9},{2,10},{3,11},{4,12},{5,13},{6,14},{7,15},{8,0},{9,1},... | collective-permute-start | bytes 393224 | tf_op jit(solution)/shard_map/ppermute | solution.py:331
  46.1 0.1 collective-permute-start.14
  46.2 2.9 %collective-permute-start.13 = (bf16[64,1024]{1,0:T(8,128)(2,1)S(1)}, bf16[64,1024]{1,0:T(8,128)(2,1)S(1)}, u32[]{:S(2)}, u32[]{:S(2)}) collective-permute-start(bf16[64,1024]{1,0:T(8,128)(2,1)S(1)} %add.7.refs_0_), channel_id=1, source_target_pairs={{0,12},{1,13},{2,14},{3,15},{4,8},{5,9},{6,10},{7,11},{8,4},{9,5},... | collective-permute-start | bytes 393224 | tf_op jit(solution)/shard_map/ppermute | solution.py:331
  49.1 2.5 %collective-permute-done.15.refs_1_ = bf16[64,1024]{1,0:T(8,128)(2,1)S(1)} collective-permute-done((bf16[64,1024]{1,0:T(8,128)(2,1)S(1)}, bf16[64,1024]{1,0:T(8,128)(2,1)S(1)}, u32[]{:S(2)}, u32[]{:S(2)}) %collective-permute-start.15) | collective-permute-done | bytes 131104 | tf_op jit(solution)/shard_map/ppermute | solution.py:331
  51.6 2.3 %collective-permute-done.14.refs_2_ = bf16[64,1024]{1,0:T(8,128)(2,1)S(1)} collective-permute-done((bf16[64,1024]{1,0:T(8,128)(2,1)S(1)}, bf16[64,1024]{1,0:T(8,128)(2,1)S(1)}, u32[]{:S(2)}, u32[]{:S(2)}) %collective-permute-start.14) | collective-permute-done | bytes 131104 | tf_op jit(solution)/shard_map/ppermute | solution.py:331
  53.9 0.0 collective-permute-done.13.refs_3_
  53.9 1.0 %to_rows.1 = f32[256,1024]{1,0:T(8,128)} custom-call(bf16[64,1024]{1,0:T(8,128)(2,1)S(1)} %add.7.refs_0_, bf16[64,1024]{1,0:T(8,128)(2,1)S(1)} %collective-permute-done.15.refs_1_, bf16[64,1024]{1,0:T(8,128)(2,1)S(1)} %collective-permute-done.14.refs_2_, bf16[64,1024]{1,0:T(8,128)(2,1)S(1)} %collective-permute-done.13.refs_3_), custom_call_target="tpu_custom_call" | custom-call | tf_op jit(solution)/shard_map/to_rows/pallas_call | solution.py:314
  (3 shorter events, 0.1 us)
Async XLA Ops:
  1.7 8.3 %collective-permute-start.3 = (bf16[4,512,512]{2,1,0:T(8,128)(2,1)}, bf16[4,512,512]{2,1,0:T(8,128)(2,1)S(1)}, u32[]{:S(2)}, u32[]{:S(2)}) collective-permute-start(bf16[4,512,512]{2,1,0:T(8,128)(2,1)} %enc_in.1), channel_id=1, source_target_pairs={{0,1},{1,0},{2,3},{3,2},{4,5},{5,4},{6,7},{7,6},{8,9},{9,8},{10,11... | collective-permute-start | bytes 6291464 | tf_op jit(solution)/shard_map/ppermute | solution.py:331
  2.2 15.1 %collective-permute-start.4 = (bf16[2,256,512]{2,1,0:T(8,128)(2,1)S(1)}, bf16[2,256,512]{2,1,0:T(8,128)(2,1)S(1)}, u32[]{:S(2)}, u32[]{:S(2)}) collective-permute-start(bf16[2,256,512]{2,1,0:T(8,128)(2,1)S(1)} %pack.1.qc_ref.refs_2_), channel_id=1, source_target_pairs={{0,2},{1,3},{2,0},{3,1},{4,6},{5,7},{6,4},{7,5},{8,10},{9,11},{10,... | collective-permute-start | bytes 1572872 | tf_op jit(solution)/shard_map/ppermute | solution.py:331
  4.8 5.2 %collective-permute-start = (s32[4]{0:T(128)}, s32[4]{0:T(128)S(1)}, u32[]{:S(2)}, u32[]{:S(2)}) collective-permute-start(s32[4]{0:T(128)} %lens_in.1), channel_id=1, source_target_pairs={{0,1},{1,0},{2,3},{3,2},{4,5},{5,4},{6,7},{7,6},{8,9},{9,8},{10,11... | collective-permute-start | bytes 56 | tf_op jit(solution)/shard_map/ppermute | solution.py:331
  4.9 5.0 %collective-permute-start.1 = (s32[4,1024]{1,0:T(4,128)}, s32[4,1024]{1,0:T(4,128)S(1)}, u32[]{:S(2)}, u32[]{:S(2)}) collective-permute-start(s32[4,1024]{1,0:T(4,128)} %beam_in.1), channel_id=1, source_target_pairs={{0,1},{1,0},{2,3},{3,2},{4,5},{5,4},{6,7},{7,6},{8,9},{9,8},{10,11... | collective-permute-start | bytes 49160 | tf_op jit(solution)/shard_map/ppermute | solution.py:331
  5.3 4.7 %collective-permute-start.2 = (f32[4,1024]{1,0:T(4,128)}, f32[4,1024]{1,0:T(4,128)S(1)}, u32[]{:S(2)}, u32[]{:S(2)}) collective-permute-start(f32[4,1024]{1,0:T(4,128)} %grad_in.1), channel_id=1, source_target_pairs={{0,1},{1,0},{2,3},{3,2},{4,5},{5,4},{6,7},{7,6},{8,9},{9,8},{10,11... | collective-permute-start | bytes 49160 | tf_op jit(solution)/shard_map/ppermute | solution.py:331
  9.9 0.5 copy-start
  14.2 8.6 %collective-permute-start.5 = (bf16[128,1024]{1,0:T(8,128)(2,1)S(1)}, bf16[128,1024]{1,0:T(8,128)(2,1)S(1)}, u32[]{:S(2)}, u32[]{:S(2)}) collective-permute-start(bf16[128,1024]{1,0:T(8,128)(2,1)S(1)} %get-tuple-element.79), channel_id=1, source_target_pairs={{0,4},{1,5},{2,6},{3,7},{4,0},{5,1},{6,2},{7,3},{8,12},{9,13},{10,... | collective-permute-start | bytes 786440 | tf_op jit(solution)/shard_map/ppermute | solution.py:331
  22.9 5.3 %collective-permute-start.8 = (bf16[64,1024]{1,0:T(8,128)(2,1)S(1)}, bf16[64,1024]{1,0:T(8,128)(2,1)S(1)}, u32[]{:S(2)}, u32[]{:S(2)}) collective-permute-start(bf16[64,1024]{1,0:T(8,128)(2,1)S(1)} %get-tuple-element.91), channel_id=1, source_target_pairs={{0,4},{1,5},{2,6},{3,7},{4,0},{5,1},{6,2},{7,3},{8,12},{9,13},{10,... | collective-permute-start | bytes 393224 | tf_op jit(solution)/shard_map/ppermute | solution.py:331
  24.7 9.3 %collective-permute-start.6 = (bf16[64,1024]{1,0:T(8,128)(2,1)S(1)}, bf16[64,1024]{1,0:T(8,128)(2,1)S(1)}, u32[]{:S(2)}, u32[]{:S(2)}) collective-permute-start(bf16[64,1024]{1,0:T(8,128)(2,1)S(1)} %get-tuple-element.88), channel_id=1, source_target_pairs={{0,10},{1,11},{2,8},{3,9},{4,14},{5,15},{6,12},{7,13},{8,2},{9,3},... | collective-permute-start | bytes 393224 | tf_op jit(solution)/shard_map/ppermute | solution.py:331
  27.3 7.8 %collective-permute-start.7 = (bf16[64,1024]{1,0:T(8,128)(2,1)S(1)}, bf16[64,1024]{1,0:T(8,128)(2,1)S(1)}, u32[]{:S(2)}, u32[]{:S(2)}) collective-permute-start(bf16[64,1024]{1,0:T(8,128)(2,1)S(1)} %get-tuple-element.89), channel_id=1, source_target_pairs={{0,14},{1,15},{2,12},{3,13},{4,10},{5,11},{6,8},{7,9},{8,6},{9,7},... | collective-permute-start | bytes 393224 | tf_op jit(solution)/shard_map/ppermute | solution.py:331
  28.2 8.0 %collective-permute-start.9 = (bf16[64,1024]{1,0:T(8,128)(2,1)S(1)}, bf16[64,1024]{1,0:T(8,128)(2,1)S(1)}, u32[]{:S(2)}, u32[]{:S(2)}) collective-permute-start(bf16[64,1024]{1,0:T(8,128)(2,1)S(1)} %add.5), channel_id=1, source_target_pairs={{0,2},{1,3},{2,0},{3,1},{4,6},{5,7},{6,4},{7,5},{8,10},{9,11},{10,... | collective-permute-start | bytes 393224 | tf_op jit(solution)/shard_map/ppermute | solution.py:331
  29.9 6.4 %collective-permute-start.10 = (bf16[64,1024]{1,0:T(8,128)(2,1)S(1)}, bf16[64,1024]{1,0:T(8,128)(2,1)S(1)}, u32[]{:S(2)}, u32[]{:S(2)}) collective-permute-start(bf16[64,1024]{1,0:T(8,128)(2,1)S(1)} %get-tuple-element.95), channel_id=1, source_target_pairs={{0,8},{1,9},{2,10},{3,11},{4,12},{5,13},{6,14},{7,15},{8,0},{9,1},... | collective-permute-start | bytes 393224 | tf_op jit(solution)/shard_map/ppermute | solution.py:331
  34.0 5.0 %collective-permute-start.11 = (bf16[4,528,512]{2,1,0:T(8,128)(2,1)S(1)}, bf16[4,528,512]{2,1,0:T(8,128)(2,1)S(1)}, u32[]{:S(2)}, u32[]{:S(2)}) collective-permute-start(bf16[4,528,512]{2,1,0:T(8,128)(2,1)S(1)} %state_away.1), channel_id=1, source_target_pairs={{0,1},{1,0},{2,3},{3,2},{4,5},{5,4},{6,7},{7,6},{8,9},{9,8},{10,11... | collective-permute-start | bytes 6488072 | tf_op jit(solution)/shard_map/ppermute | solution.py:331
  36.3 9.2 %collective-permute-start.12 = (bf16[64,1024]{1,0:T(8,128)(2,1)S(1)}, bf16[64,1024]{1,0:T(8,128)(2,1)S(1)}, u32[]{:S(2)}, u32[]{:S(2)}) collective-permute-start(bf16[64,1024]{1,0:T(8,128)(2,1)S(1)} %add.6.refs_0_), channel_id=1, source_target_pairs={{0,16},{1,17},{2,18},{3,19},{4,20},{5,21},{6,22},{7,23},{8,24},{9,... | collective-permute-start | bytes 393224 | tf_op jit(solution)/shard_map/ppermute | solution.py:331
  45.5 6.1 %collective-permute-start.15 = (bf16[64,1024]{1,0:T(8,128)(2,1)S(1)}, bf16[64,1024]{1,0:T(8,128)(2,1)S(1)}, u32[]{:S(2)}, u32[]{:S(2)}) collective-permute-start(bf16[64,1024]{1,0:T(8,128)(2,1)S(1)} %add.7.refs_0_), channel_id=1, source_target_pairs={{0,8},{1,9},{2,10},{3,11},{4,12},{5,13},{6,14},{7,15},{8,0},{9,1},... | collective-permute-start | bytes 393224 | tf_op jit(solution)/shard_map/ppermute | solution.py:331
  46.1 7.8 %collective-permute-start.14 = (bf16[64,1024]{1,0:T(8,128)(2,1)S(1)}, bf16[64,1024]{1,0:T(8,128)(2,1)S(1)}, u32[]{:S(2)}, u32[]{:S(2)}) collective-permute-start(bf16[64,1024]{1,0:T(8,128)(2,1)S(1)} %add.7.refs_0_), channel_id=1, source_target_pairs={{0,4},{1,5},{2,6},{3,7},{4,0},{5,1},{6,2},{7,3},{8,12},{9,13},{10,... | collective-permute-start | bytes 393224 | tf_op jit(solution)/shard_map/ppermute | solution.py:331
  46.2 7.7 %collective-permute-start.13 = (bf16[64,1024]{1,0:T(8,128)(2,1)S(1)}, bf16[64,1024]{1,0:T(8,128)(2,1)S(1)}, u32[]{:S(2)}, u32[]{:S(2)}) collective-permute-start(bf16[64,1024]{1,0:T(8,128)(2,1)S(1)} %add.7.refs_0_), channel_id=1, source_target_pairs={{0,12},{1,13},{2,14},{3,15},{4,8},{5,9},{6,10},{7,11},{8,4},{9,5},... | collective-permute-start | bytes 393224 | tf_op jit(solution)/shard_map/ppermute | solution.py:331

commit v2 on v1

--- a/solution.py
+++ b/solution.py
@@ -298,10 +298,11 @@
 def rows_kernel(*refs):
     block_refs, (out_ref, rows_ref, sem) = refs[:-3], refs[-3:]
     size = block_refs[0].shape[0]
+    core = lax.axis_index("blk") & 1
     copies = []
-    for i, ref in enumerate(block_refs):
+    for i, (ref, block) in enumerate(zip(block_refs, (0, 1 + core, 2 - core, 3))):
         rows_ref[i] = ref[...].astype(F32)
-        to = pl.ds(pl.multiple_of((turn() ^ i) * size, size), size)
+        to = pl.ds(pl.multiple_of((turn() ^ block) * size, size), size)
         copies.append(pltpu.make_async_copy(rows_ref.at[i], out_ref.at[to], sem.at[i]))
         copies[-1].start()
     for copy in copies:
@@ -327,8 +328,9 @@
     docs, tokens, _ = encoded.shape
     total = reps * blks
 
-    def swap(x, mask):
-        return lax.ppermute(x, ("rep", "blk"), [(i, i ^ mask) for i in range(total)])
+    def swap(x, mask, other=None):
+        masks = (mask, mask if other is None else other)
+        return lax.ppermute(x, ("rep", "blk"), [(i, i ^ masks[i & 1]) for i in range(total)])
 
     core, ax = 1, 2
     ay, az, azz = blks, 2 * blks, 4 * blks
@@ -404,7 +406,9 @@
         members = [[i * 8 + j for i in range(reps // 8)] for j in range(8)]
         own = lax.psum(own.astype(F32), "rep", axis_index_groups=members).astype(BF16)
 
-    both, second, first = lax.optimization_barrier([swap(own, mask) for mask in turns[:0:-1]])
+    both, second, first = lax.optimization_barrier(
+        [swap(own, ay | az), swap(own, ay, az), swap(own, az, ay)]
+    )
     label_grad = to_rows([own, first, second, both])
     return logits, state, label_grad
 

time: 55.3 us -> 55.4 us (level)
  no operation moved by 1% of the time
where the time goes in v2:
time: 55.4 us; the launch traced here: 55.2 us
  Pallas kernels  22.5 us (41%)
  starting transfers between devices  19.3 us (35%)
  waiting for transfers between devices  12 us (22%)
  between operations  0.92 us (2%)
    ppermute x16, starting transfers between devices, swap(): lax.ppermute(x, ('rep', 'blk'), [(i, i ^ masks[i & 1]) for i in range(tot...  19.3 us
    pallas_call x9, Pallas kernels, call(): pl.pallas_call(kernel, out_shape=out_shape, in_specs=[HBM if i < hbm else...  17.5 us
    ppermute x16, waiting for transfers between devices, swap(): lax.ppermute(x, ('rep', 'blk'), [(i, i ^ masks[i & 1]) for i in range(tot...  12 us
    pallas_call x1, Pallas kernels, state_grad(): pl.pallas_call(functools.partial(home_kernel, (0, 2)), out_shape=[out, sh...  3.99 us
  transfers between devices with their start and end apart: 16, of which 7 were waited for; matrix products, arithmetic and copies ran while one was open for 0% of the time, Pallas kernels for 37%

profile of v2, /device:TPU:0, one launch (start us, length us, event | category | flops | bytes accessed | tf_op | source)
XLA Modules:
  0.0 55.2 jit_solution(339147806686631804)
XLA Ops:
  0.6 1.0 %pack.1.qc_ref.refs_2_ = bf16[2,256,512]{2,1,0:T(8,128)(2,1)S(1)} custom-call(bf16[256,512]{1,0:T(8,128)(2,1)} %q_in.1, bf16[256,512]{1,0:T(8,128)(2,1)} %c_in.1), custom_call_target="tpu_custom_call" | custom-call | tf_op jit(solution)/shard_map/pack/pallas_call | solution.py:43
  1.7 0.5 collective-permute-start.3
  2.2 2.6 %collective-permute-start.4 = (bf16[2,256,512]{2,1,0:T(8,128)(2,1)S(1)}, bf16[2,256,512]{2,1,0:T(8,128)(2,1)S(1)}, u32[]{:S(2)}, u32[]{:S(2)}) collective-permute-start(bf16[2,256,512]{2,1,0:T(8,128)(2,1)S(1)} %pack.1.qc_ref.refs_2_), channel_id=1, source_target_pairs={{0,2},{1,3},{2,0},{3,1},{4,6},{5,7},{6,4},{7,5},{8,10},{9,11},{10,... | collective-permute-start | bytes 1572872 | tf_op jit(solution)/shard_map/ppermute | solution.py:333
  4.8 0.2 collective-permute-start
  4.9 0.3 collective-permute-start.1
  5.3 0.2 collective-permute-start.2
  5.4 4.5 %own_labels.1 = (bf16[4,512,512]{2,1,0:T(8,128)(2,1)S(1)}, f32[4,1152]{1,0:T(4,128)S(1)}, bf16[4,512,512]{2,1,0:T(8,128)(2,1)S(1)}, bf16[4,512,256]{2,1,0:T(8,12...) custom-call(bf16[4,512,512]{2,1,0:T(8,128)(2,1)} %enc_in.1, ...), custom_call_target="tpu_custom_call" | custom-call | flops 2147483648 | bytes 4194304 | tf_op jit(solution)/shard_map/own_labels/pallas_call | solution.py:43
  9.9 0.0 collective-permute-done.lens_in
  9.9 0.0 copy-start
  10.0 0.0 collective-permute-done.1.beam_ref
  10.0 0.0 collective-permute-done.2.grad_ref
  10.0 0.0 collective-permute-done.3.enc_ref.enc2_ref
  10.0 0.5 copy-done
  10.5 3.7 %own_labels_other_docs.1 = (f32[4,1152]{1,0:T(4,128)S(1)}, bf16[4,512,512]{2,1,0:T(8,128)(2,1)S(1)}, bf16[4,512,256]{2,1,0:T(8,128)(2,1)S(1)}, bf16[4,512,256]{2...) custom-call(s32[4]{0:T(128)} %copy-done, ...), custom_call_target="tpu_custom_call" | custom-call | flops 2147483648 | bytes 4194304 | tf_op jit(solution)/shard_map/own_labels_other_docs/pallas_call | solution.py:43
  14.2 1.6 %collective-permute-start.5 = (bf16[128,1024]{1,0:T(8,128)(2,1)S(1)}, bf16[128,1024]{1,0:T(8,128)(2,1)S(1)}, u32[]{:S(2)}, u32[]{:S(2)}) collective-permute-start(bf16[128,1024]{1,0:T(8,128)(2,1)S(1)} %get-tuple-element.79), channel_id=1, source_target_pairs={{0,4},{1,5},{2,6},{3,7},{4,0},{5,1},{6,2},{7,3},{8,12},{9,13},{10,... | collective-permute-start | bytes 786440 | tf_op jit(solution)/shard_map/ppermute | solution.py:333
  15.8 1.5 %collective-permute-done.4.qc_ref.refs_6_ = bf16[2,256,512]{2,1,0:T(8,128)(2,1)S(1)} collective-permute-done((bf16[2,256,512]{2,1,0:T(8,128)(2,1)S(1)}, bf16[2,256,512]{2,1,0:T(8,128)(2,1)S(1)}, u32[]{:S(2)}, u32[]{:S(2)}) %collective-permute-start.4) | collective-permute-done | bytes 524320 | tf_op jit(solution)/shard_map/ppermute | solution.py:333
  17.3 5.5 %far_labels.1 = (bf16[4,512,256]{2,1,0:T(8,128)(2,1)S(1)}, bf16[4,512,256]{2,1,0:T(8,128)(2,1)S(1)}, f32[4,256]{1,0:T(4,128)S(1)}, bf16[4,512,256]{2,1,0:T(8,128...) custom-call(f32[4,1152]{1,0:T(4,128)S(1)} %get-tuple-element.61.gate, ...), custom_call_target="tpu_custom_call" | custom-call | flops 4294967296 | bytes 8388608 | tf_op jit(solution)/shard_map/far_labels/pallas_call | solution.py:43
  22.8 0.0 collective-permute-done.5.refs_1_
  22.9 1.8 %collective-permute-start.8 = (bf16[64,1024]{1,0:T(8,128)(2,1)S(1)}, bf16[64,1024]{1,0:T(8,128)(2,1)S(1)}, u32[]{:S(2)}, u32[]{:S(2)}) collective-permute-start(bf16[64,1024]{1,0:T(8,128)(2,1)S(1)} %get-tuple-element.91), channel_id=1, source_target_pairs={{0,4},{1,5},{2,6},{3,7},{4,0},{5,1},{6,2},{7,3},{8,12},{9,13},{10,... | collective-permute-start | bytes 393224 | tf_op jit(solution)/shard_map/ppermute | solution.py:333
  24.7 2.5 %collective-permute-start.6 = (bf16[64,1024]{1,0:T(8,128)(2,1)S(1)}, bf16[64,1024]{1,0:T(8,128)(2,1)S(1)}, u32[]{:S(2)}, u32[]{:S(2)}) collective-permute-start(bf16[64,1024]{1,0:T(8,128)(2,1)S(1)} %get-tuple-element.88), channel_id=1, source_target_pairs={{0,10},{1,11},{2,8},{3,9},{4,14},{5,15},{6,12},{7,13},{8,2},{9,3},... | collective-permute-start | bytes 393224 | tf_op jit(solution)/shard_map/ppermute | solution.py:333
  27.3 0.1 collective-permute-start.7
  27.3 0.8 %collective-permute-done.8.refs_1_ = bf16[64,1024]{1,0:T(8,128)(2,1)S(1)} collective-permute-done((bf16[64,1024]{1,0:T(8,128)(2,1)S(1)}, bf16[64,1024]{1,0:T(8,128)(2,1)S(1)}, u32[]{:S(2)}, u32[]{:S(2)}) %collective-permute-start.8) | collective-permute-done | bytes 131104 | tf_op jit(solution)/shard_map/ppermute | solution.py:333
  28.2 1.6 %collective-permute-start.9 = (bf16[64,1024]{1,0:T(8,128)(2,1)S(1)}, bf16[64,1024]{1,0:T(8,128)(2,1)S(1)}, u32[]{:S(2)}, u32[]{:S(2)}) collective-permute-start(bf16[64,1024]{1,0:T(8,128)(2,1)S(1)} %add.5), channel_id=1, source_target_pairs={{0,2},{1,3},{2,0},{3,1},{4,6},{5,7},{6,4},{7,5},{8,10},{9,11},{10,... | collective-permute-start | bytes 393224 | tf_op jit(solution)/shard_map/ppermute | solution.py:333
  29.9 1.6 %collective-permute-start.10 = (bf16[64,1024]{1,0:T(8,128)(2,1)S(1)}, bf16[64,1024]{1,0:T(8,128)(2,1)S(1)}, u32[]{:S(2)}, u32[]{:S(2)}) collective-permute-start(bf16[64,1024]{1,0:T(8,128)(2,1)S(1)} %get-tuple-element.95), channel_id=1, source_target_pairs={{0,8},{1,9},{2,10},{3,11},{4,12},{5,13},{6,14},{7,15},{8,0},{9,1},... | collective-permute-start | bytes 393224 | tf_op jit(solution)/shard_map/ppermute | solution.py:333
  31.5 2.5 %state_away.1 = bf16[4,528,512]{2,1,0:T(8,128)(2,1)S(1)} custom-call(f32[4,1152]{1,0:T(4,128)S(1)} %get-tuple-element.68.gate2_ref.gate_ref, bf16[4,512,256]{2,1,0:T(8,128)(2,1)S(1)} %get-tuple-element.103.refs_0_, bf16[4,512,256]{2,1,0:T(8,128)(2,1)S(1)} %get-tuple-element.104.refs_1_, bf16[2,256,512]{2,1,0:T(8,128)(2,1)S(1)} %pack.1.qc_ref.refs_2_, ...), custom_call_target="tpu_custom_call" | custom-call | flops 2147483648 | bytes 4194304 | tf_op jit(solution)/shard_map/state_away/pallas_call | solution.py:43
  34.0 0.1 collective-permute-start.11
  34.1 0.0 collective-permute-done.6.refs_2_
  34.1 1.0 %collective-permute-done.7.refs_3_ = bf16[64,1024]{1,0:T(8,128)(2,1)S(1)} collective-permute-done((bf16[64,1024]{1,0:T(8,128)(2,1)S(1)}, bf16[64,1024]{1,0:T(8,128)(2,1)S(1)}, u32[]{:S(2)}, u32[]{:S(2)}) %collective-permute-start.7) | collective-permute-done | bytes 131104 | tf_op jit(solution)/shard_map/ppermute | solution.py:333
  35.1 1.2 %collective-permute-done.9.refs_4_ = bf16[64,1024]{1,0:T(8,128)(2,1)S(1)} collective-permute-done((bf16[64,1024]{1,0:T(8,128)(2,1)S(1)}, bf16[64,1024]{1,0:T(8,128)(2,1)S(1)}, u32[]{:S(2)}, u32[]{:S(2)}) %collective-permute-start.9) | collective-permute-done | bytes 131104 | tf_op jit(solution)/shard_map/ppermute | solution.py:333
  36.2 0.0 collective-permute-done.10.refs_1_
  36.2 0.1 add.6.refs_0_
  36.3 2.7 %collective-permute-start.12 = (bf16[64,1024]{1,0:T(8,128)(2,1)S(1)}, bf16[64,1024]{1,0:T(8,128)(2,1)S(1)}, u32[]{:S(2)}, u32[]{:S(2)}) collective-permute-start(bf16[64,1024]{1,0:T(8,128)(2,1)S(1)} %add.6.refs_0_), channel_id=1, source_target_pairs={{0,16},{1,17},{2,18},{3,19},{4,20},{5,21},{6,22},{7,23},{8,24},{9,... | collective-permute-start | bytes 393224 | tf_op jit(solution)/shard_map/ppermute | solution.py:333
  39.0 0.0 collective-permute-done.11.refs_8_
  39.0 4.0 %state_home.1 = (bf16[4,512,512]{2,1,0:T(8,128)(2,1)}, f32[4,1024]{1,0:T(4,128)}) custom-call(f32[4,1152]{1,0:T(4,128)S(1)} %get-tuple-element.61.gate_ref, bf16[4,512,256]{2,1,0:T(8,128)(2,1)S(1)} %get-tuple-element.62.refs_0_, bf16[4,512,256]{2,1,0:T(8,128)(2,1)S(1)} %get-tuple-element.63.refs_1_, bf16[2,256,512]{2,1,0:T(8,128)(2,1)S(1)} %pack.1.qc_ref.refs_2_, ...), custom_call_target="tpu_custom_call" | custom-call | flops 2147483648 | bytes 4194304 | tf_op jit(solution)/shard_map/state_home/pallas_call | solution.py:269
  43.0 2.5 %collective-permute-done.12.refs_1_ = bf16[64,1024]{1,0:T(8,128)(2,1)S(1)} collective-permute-done((bf16[64,1024]{1,0:T(8,128)(2,1)S(1)}, bf16[64,1024]{1,0:T(8,128)(2,1)S(1)}, u32[]{:S(2)}, u32[]{:S(2)}) %collective-permute-start.12) | collective-permute-done | bytes 131104 | tf_op jit(solution)/shard_map/ppermute | solution.py:333
  45.5 0.6 %collective-permute-start.15 = (bf16[64,1024]{1,0:T(8,128)(2,1)S(1)}, bf16[64,1024]{1,0:T(8,128)(2,1)S(1)}, u32[]{:S(2)}, u32[]{:S(2)}) collective-permute-start(bf16[64,1024]{1,0:T(8,128)(2,1)S(1)} %add.7.refs_0_), channel_id=1, source_target_pairs={{0,8},{1,5},{2,10},{3,7},{4,12},{5,1},{6,14},{7,3},{8,0},{9,13},{1... | collective-permute-start | bytes 393224 | tf_op jit(solution)/shard_map/ppermute | solution.py:333
  46.1 0.1 collective-permute-start.14
  46.2 2.9 %collective-permute-start.13 = (bf16[64,1024]{1,0:T(8,128)(2,1)S(1)}, bf16[64,1024]{1,0:T(8,128)(2,1)S(1)}, u32[]{:S(2)}, u32[]{:S(2)}) collective-permute-start(bf16[64,1024]{1,0:T(8,128)(2,1)S(1)} %add.7.refs_0_), channel_id=1, source_target_pairs={{0,12},{1,13},{2,14},{3,15},{4,8},{5,9},{6,10},{7,11},{8,4},{9,5},... | collective-permute-start | bytes 393224 | tf_op jit(solution)/shard_map/ppermute | solution.py:333
  49.1 2.5 %collective-permute-done.15.refs_1_ = bf16[64,1024]{1,0:T(8,128)(2,1)S(1)} collective-permute-done((bf16[64,1024]{1,0:T(8,128)(2,1)S(1)}, bf16[64,1024]{1,0:T(8,128)(2,1)S(1)}, u32[]{:S(2)}, u32[]{:S(2)}) %collective-permute-start.15) | collective-permute-done | bytes 131104 | tf_op jit(solution)/shard_map/ppermute | solution.py:333
  51.6 0.0 collective-permute-done.14.refs_2_
  51.6 2.4 %collective-permute-done.13.refs_3_ = bf16[64,1024]{1,0:T(8,128)(2,1)S(1)} collective-permute-done((bf16[64,1024]{1,0:T(8,128)(2,1)S(1)}, bf16[64,1024]{1,0:T(8,128)(2,1)S(1)}, u32[]{:S(2)}, u32[]{:S(2)}) %collective-permute-start.13) | collective-permute-done | bytes 131104 | tf_op jit(solution)/shard_map/ppermute | solution.py:333
  54.1 1.0 %to_rows.1 = f32[256,1024]{1,0:T(8,128)} custom-call(bf16[64,1024]{1,0:T(8,128)(2,1)S(1)} %add.7.refs_0_, bf16[64,1024]{1,0:T(8,128)(2,1)S(1)} %collective-permute-done.15.refs_1_, bf16[64,1024]{1,0:T(8,128)(2,1)S(1)} %collective-permute-done.14.refs_2_, bf16[64,1024]{1,0:T(8,128)(2,1)S(1)} %collective-permute-done.13.refs_3_), custom_call_target="tpu_custom_call" | custom-call | tf_op jit(solution)/shard_map/to_rows/pallas_call | solution.py:315
  (3 shorter events, 0.1 us)
Async XLA Ops:
  1.7 8.3 %collective-permute-start.3 = (bf16[4,512,512]{2,1,0:T(8,128)(2,1)}, bf16[4,512,512]{2,1,0:T(8,128)(2,1)S(1)}, u32[]{:S(2)}, u32[]{:S(2)}) collective-permute-start(bf16[4,512,512]{2,1,0:T(8,128)(2,1)} %enc_in.1), channel_id=1, source_target_pairs={{0,1},{1,0},{2,3},{3,2},{4,5},{5,4},{6,7},{7,6},{8,9},{9,8},{10,11... | collective-permute-start | bytes 6291464 | tf_op jit(solution)/shard_map/ppermute | solution.py:333
  2.2 15.1 %collective-permute-start.4 = (bf16[2,256,512]{2,1,0:T(8,128)(2,1)S(1)}, bf16[2,256,512]{2,1,0:T(8,128)(2,1)S(1)}, u32[]{:S(2)}, u32[]{:S(2)}) collective-permute-start(bf16[2,256,512]{2,1,0:T(8,128)(2,1)S(1)} %pack.1.qc_ref.refs_2_), channel_id=1, source_target_pairs={{0,2},{1,3},{2,0},{3,1},{4,6},{5,7},{6,4},{7,5},{8,10},{9,11},{10,... | collective-permute-start | bytes 1572872 | tf_op jit(solution)/shard_map/ppermute | solution.py:333
  4.8 5.2 %collective-permute-start = (s32[4]{0:T(128)}, s32[4]{0:T(128)S(1)}, u32[]{:S(2)}, u32[]{:S(2)}) collective-permute-start(s32[4]{0:T(128)} %lens_in.1), channel_id=1, source_target_pairs={{0,1},{1,0},{2,3},{3,2},{4,5},{5,4},{6,7},{7,6},{8,9},{9,8},{10,11... | collective-permute-start | bytes 56 | tf_op jit(solution)/shard_map/ppermute | solution.py:333
  4.9 5.0 %collective-permute-start.1 = (s32[4,1024]{1,0:T(4,128)}, s32[4,1024]{1,0:T(4,128)S(1)}, u32[]{:S(2)}, u32[]{:S(2)}) collective-permute-start(s32[4,1024]{1,0:T(4,128)} %beam_in.1), channel_id=1, source_target_pairs={{0,1},{1,0},{2,3},{3,2},{4,5},{5,4},{6,7},{7,6},{8,9},{9,8},{10,11... | collective-permute-start | bytes 49160 | tf_op jit(solution)/shard_map/ppermute | solution.py:333
  5.3 4.7 %collective-permute-start.2 = (f32[4,1024]{1,0:T(4,128)}, f32[4,1024]{1,0:T(4,128)S(1)}, u32[]{:S(2)}, u32[]{:S(2)}) collective-permute-start(f32[4,1024]{1,0:T(4,128)} %grad_in.1), channel_id=1, source_target_pairs={{0,1},{1,0},{2,3},{3,2},{4,5},{5,4},{6,7},{7,6},{8,9},{9,8},{10,11... | collective-permute-start | bytes 49160 | tf_op jit(solution)/shard_map/ppermute | solution.py:333
  9.9 0.5 copy-start
  14.2 8.6 %collective-permute-start.5 = (bf16[128,1024]{1,0:T(8,128)(2,1)S(1)}, bf16[128,1024]{1,0:T(8,128)(2,1)S(1)}, u32[]{:S(2)}, u32[]{:S(2)}) collective-permute-start(bf16[128,1024]{1,0:T(8,128)(2,1)S(1)} %get-tuple-element.79), channel_id=1, source_target_pairs={{0,4},{1,5},{2,6},{3,7},{4,0},{5,1},{6,2},{7,3},{8,12},{9,13},{10,... | collective-permute-start | bytes 786440 | tf_op jit(solution)/shard_map/ppermute | solution.py:333
  22.9 5.3 %collective-permute-start.8 = (bf16[64,1024]{1,0:T(8,128)(2,1)S(1)}, bf16[64,1024]{1,0:T(8,128)(2,1)S(1)}, u32[]{:S(2)}, u32[]{:S(2)}) collective-permute-start(bf16[64,1024]{1,0:T(8,128)(2,1)S(1)} %get-tuple-element.91), channel_id=1, source_target_pairs={{0,4},{1,5},{2,6},{3,7},{4,0},{5,1},{6,2},{7,3},{8,12},{9,13},{10,... | collective-permute-start | bytes 393224 | tf_op jit(solution)/shard_map/ppermute | solution.py:333
  24.7 9.3 %collective-permute-start.6 = (bf16[64,1024]{1,0:T(8,128)(2,1)S(1)}, bf16[64,1024]{1,0:T(8,128)(2,1)S(1)}, u32[]{:S(2)}, u32[]{:S(2)}) collective-permute-start(bf16[64,1024]{1,0:T(8,128)(2,1)S(1)} %get-tuple-element.88), channel_id=1, source_target_pairs={{0,10},{1,11},{2,8},{3,9},{4,14},{5,15},{6,12},{7,13},{8,2},{9,3},... | collective-permute-start | bytes 393224 | tf_op jit(solution)/shard_map/ppermute | solution.py:333
  27.3 7.8 %collective-permute-start.7 = (bf16[64,1024]{1,0:T(8,128)(2,1)S(1)}, bf16[64,1024]{1,0:T(8,128)(2,1)S(1)}, u32[]{:S(2)}, u32[]{:S(2)}) collective-permute-start(bf16[64,1024]{1,0:T(8,128)(2,1)S(1)} %get-tuple-element.89), channel_id=1, source_target_pairs={{0,14},{1,15},{2,12},{3,13},{4,10},{5,11},{6,8},{7,9},{8,6},{9,7},... | collective-permute-start | bytes 393224 | tf_op jit(solution)/shard_map/ppermute | solution.py:333
  28.2 8.0 %collective-permute-start.9 = (bf16[64,1024]{1,0:T(8,128)(2,1)S(1)}, bf16[64,1024]{1,0:T(8,128)(2,1)S(1)}, u32[]{:S(2)}, u32[]{:S(2)}) collective-permute-start(bf16[64,1024]{1,0:T(8,128)(2,1)S(1)} %add.5), channel_id=1, source_target_pairs={{0,2},{1,3},{2,0},{3,1},{4,6},{5,7},{6,4},{7,5},{8,10},{9,11},{10,... | collective-permute-start | bytes 393224 | tf_op jit(solution)/shard_map/ppermute | solution.py:333
  29.9 6.4 %collective-permute-start.10 = (bf16[64,1024]{1,0:T(8,128)(2,1)S(1)}, bf16[64,1024]{1,0:T(8,128)(2,1)S(1)}, u32[]{:S(2)}, u32[]{:S(2)}) collective-permute-start(bf16[64,1024]{1,0:T(8,128)(2,1)S(1)} %get-tuple-element.95), channel_id=1, source_target_pairs={{0,8},{1,9},{2,10},{3,11},{4,12},{5,13},{6,14},{7,15},{8,0},{9,1},... | collective-permute-start | bytes 393224 | tf_op jit(solution)/shard_map/ppermute | solution.py:333
  34.0 5.0 %collective-permute-start.11 = (bf16[4,528,512]{2,1,0:T(8,128)(2,1)S(1)}, bf16[4,528,512]{2,1,0:T(8,128)(2,1)S(1)}, u32[]{:S(2)}, u32[]{:S(2)}) collective-permute-start(bf16[4,528,512]{2,1,0:T(8,128)(2,1)S(1)} %state_away.1), channel_id=1, source_target_pairs={{0,1},{1,0},{2,3},{3,2},{4,5},{5,4},{6,7},{7,6},{8,9},{9,8},{10,11... | collective-permute-start | bytes 6488072 | tf_op jit(solution)/shard_map/ppermute | solution.py:333
  36.3 9.2 %collective-permute-start.12 = (bf16[64,1024]{1,0:T(8,128)(2,1)S(1)}, bf16[64,1024]{1,0:T(8,128)(2,1)S(1)}, u32[]{:S(2)}, u32[]{:S(2)}) collective-permute-start(bf16[64,1024]{1,0:T(8,128)(2,1)S(1)} %add.6.refs_0_), channel_id=1, source_target_pairs={{0,16},{1,17},{2,18},{3,19},{4,20},{5,21},{6,22},{7,23},{8,24},{9,... | collective-permute-start | bytes 393224 | tf_op jit(solution)/shard_map/ppermute | solution.py:333
  45.5 6.1 %collective-permute-start.15 = (bf16[64,1024]{1,0:T(8,128)(2,1)S(1)}, bf16[64,1024]{1,0:T(8,128)(2,1)S(1)}, u32[]{:S(2)}, u32[]{:S(2)}) collective-permute-start(bf16[64,1024]{1,0:T(8,128)(2,1)S(1)} %add.7.refs_0_), channel_id=1, source_target_pairs={{0,8},{1,5},{2,10},{3,7},{4,12},{5,1},{6,14},{7,3},{8,0},{9,13},{1... | collective-permute-start | bytes 393224 | tf_op jit(solution)/shard_map/ppermute | solution.py:333
  46.1 5.5 %collective-permute-start.14 = (bf16[64,1024]{1,0:T(8,128)(2,1)S(1)}, bf16[64,1024]{1,0:T(8,128)(2,1)S(1)}, u32[]{:S(2)}, u32[]{:S(2)}) collective-permute-start(bf16[64,1024]{1,0:T(8,128)(2,1)S(1)} %add.7.refs_0_), channel_id=1, source_target_pairs={{0,4},{1,9},{2,6},{3,11},{4,0},{5,13},{6,2},{7,15},{8,12},{9,1},{1... | collective-permute-start | bytes 393224 | tf_op jit(solution)/shard_map/ppermute | solution.py:333
  46.2 7.8 %collective-permute-start.13 = (bf16[64,1024]{1,0:T(8,128)(2,1)S(1)}, bf16[64,1024]{1,0:T(8,128)(2,1)S(1)}, u32[]{:S(2)}, u32[]{:S(2)}) collective-permute-start(bf16[64,1024]{1,0:T(8,128)(2,1)S(1)} %add.7.refs_0_), channel_id=1, source_target_pairs={{0,12},{1,13},{2,14},{3,15},{4,8},{5,9},{6,10},{7,11},{8,4},{9,5},... | collective-permute-start | bytes 393224 | tf_op jit(solution)/shard_map/ppermute | solution.py:333
